TPU v7x, 128 devices: a whole 4x4x4 slice. The times are simulated.
128 devices in a mesh: rep: 8 (over y_lo, x), tp: 16 (over z, y_hi, core).
Axes of the slice: x: 4, y: 4 (y_hi: 2, y_lo: 2; y = y_hi * 2 + y_lo), z: 4, core: 2. Of those that a mesh axis runs over, the one named last changes fastest.
Arguments:
- hidden: bfloat16 [4, 1024, 8192], P(None, 'rep'), may hold values from -64 to 64
- norm_gain: bfloat16 [8192], replicated, may hold values from 0.099609375 to 1.8984375
- q_weight: bfloat16 [8192, 8192], P(('rep', 'tp')), may hold values from -0.0625 to 0.0625
- k_weight: bfloat16 [8192, 1024], P(('rep', 'tp')), may hold values from -0.0625 to 0.0625
- v_weight: bfloat16 [8192, 1024], P(('rep', 'tp')), may hold values from -0.0625 to 0.0625
- o_weight: bfloat16 [8192, 8192], P(('tp', 'rep')), may hold values from -0.0625 to 0.0625
- key_cache: bfloat16 [1024, 16, 192, 128], P('rep', 'tp'), may hold values from -256 to 256, as said below
- value_cache: bfloat16 [1024, 16, 192, 128], P('rep', 'tp'), may hold values from -8 to 8, as said below
- cache_len: int32 [1024], P('rep'), may hold values from 2 to 192
- finish: int32 [1024], P('rep'), may hold values from 0 to 4
- owner: int32 [1024, 1], P('rep'), may hold values from 0 to 127; in each aligned block of 128 rows (0 to 127, 128 to 255, ...) at most 2 rows name the same one
Outputs:
- decoded: bfloat16 [4, 1024, 8192], P(None, 'rep', 'tp')
- returned: bfloat16 [2048, 8192], P(('rep', 'tp'))
Inputs may be any that keep to these rules, and one draw needn't show every extreme that they name: At most 2 rows of one replica, that is of one aligned block of 128 rows, have the same owner. `key_cache`: copies j = 0 to 1 of one key head are equal. `value_cache`: copies j = 0 to 1 of one value head are equal.
All inputs are finite; a program needn't handle non-finite values.
Results may differ from a plain program's by a relative error of at most 0.008.
Values may be sent and summed in bfloat16 or wider, within the bound.
A program may use at most 192 MiB of HBM per device.

v0:
```python
import jax
import jax.numpy as jnp
from jax import lax
from jax.sharding import PartitionSpec as P

KV = 8


def rotate_half(values, angles):
    half = values.shape[-1] // 2
    first = values[..., :half]
    second = values[..., half:]
    cosine = jnp.cos(angles)
    sine = jnp.sin(angles)
    return jnp.concatenate(
        [first * cosine - second * sine, second * cosine + first * sine], axis=-1
    )


def per_device(
    hidden,
    norm_gain,
    q_weight,
    k_weight,
    v_weight,
    o_weight,
    key_cache,
    value_cache,
    cache_len,
    finish,
    owner,
):
    tp_count = lax.axis_size("tp")
    rep_count = lax.axis_size("rep")
    tp_index = lax.axis_index("tp")
    step_count, row_count, model_width = hidden.shape
    head_size = key_cache.shape[-1]
    cache_size = key_cache.shape[2]
    local_rows = q_weight.shape[0]
    share = model_width // tp_count
    pair_weight = jnp.concatenate(
        [
            k_weight.reshape(local_rows, KV, 1, head_size),
            v_weight.reshape(local_rows, KV, 1, head_size),
        ],
        axis=2,
    )
    kv_spread = jnp.repeat(pair_weight, tp_count // KV, axis=1).reshape(
        local_rows, tp_count * 2 * head_size
    )
    query_part, kv_part = (
        lax.all_to_all(q_weight, "tp", split_axis=1, concat_axis=0, tiled=True),
        lax.all_to_all(kv_spread, "tp", split_axis=1, concat_axis=0, tiled=True),
    )
    hidden_f = hidden.astype(jnp.float32)
    mean_square = jnp.mean(hidden_f * hidden_f, axis=-1, keepdims=True)
    normed = (hidden_f * lax.rsqrt(mean_square + 1e-05) * norm_gain.astype(jnp.float32)).astype(
        jnp.bfloat16
    )
    token_count = step_count * row_count
    normed_flat = normed.reshape(token_count, model_width)
    query_full, kv_full = (
        lax.all_gather(query_part, "rep", axis=0, tiled=True),
        lax.all_gather(kv_part, "rep", axis=0, tiled=True),
    )
    query_proj = jnp.dot(normed_flat, query_full, preferred_element_type=jnp.float32)
    kv_proj = jnp.dot(normed_flat, kv_full, preferred_element_type=jnp.float32)
    heads_here = query_proj.shape[1] // head_size
    positions = cache_len[None, :] + jnp.arange(step_count, dtype=jnp.int32)[:, None]
    half = head_size // 2
    freqs = 500000.0 ** (-(jnp.arange(half, dtype=jnp.float32) * 2.0) / head_size)
    angles = (positions.astype(jnp.float32)[..., None] * freqs).reshape(token_count, 1, half)
    query_rot = rotate_half(query_proj.reshape(token_count, heads_here, head_size), angles).astype(
        jnp.bfloat16
    )
    key_rot = rotate_half(kv_proj[:, :head_size], angles[:, 0, :]).astype(jnp.bfloat16)
    value_new = kv_proj[:, head_size:].astype(jnp.bfloat16)
    query_rows = query_rot.reshape(step_count, row_count, heads_here, head_size).transpose(
        1, 0, 2, 3
    )
    query_rows = query_rows.reshape(row_count, step_count * heads_here, head_size)
    key_rows = key_rot.reshape(step_count, row_count, head_size).transpose(1, 0, 2)
    value_rows = value_new.reshape(step_count, row_count, head_size).transpose(1, 0, 2)
    key_old = key_cache[:, 0]
    value_old = value_cache[:, 0]
    scale = 1.0 / jnp.sqrt(jnp.float32(head_size))
    old_scores = (
        jnp.einsum("rqd,rjd->rqj", query_rows, key_old, preferred_element_type=jnp.float32) * scale
    )
    new_scores = (
        jnp.einsum("rqd,rtd->rqt", query_rows, key_rows, preferred_element_type=jnp.float32) * scale
    )
    old_mask = jnp.arange(cache_size)[None, None, :] < cache_len[:, None, None]
    query_step = jnp.arange(step_count * heads_here) // heads_here
    new_mask = (jnp.arange(step_count)[None, :] <= query_step[:, None])[None, :, :]
    old_scores = jnp.where(old_mask, old_scores, -jnp.inf)
    new_scores = jnp.where(new_mask, new_scores, -jnp.inf)
    top = jnp.maximum(
        jnp.max(old_scores, -1, keepdims=True), jnp.max(new_scores, -1, keepdims=True)
    )
    old_exp = jnp.exp(old_scores - top)
    new_exp = jnp.exp(new_scores - top)
    total = jnp.sum(old_exp, -1, keepdims=True) + jnp.sum(new_exp, -1, keepdims=True)
    old_probs = (old_exp / total).astype(jnp.bfloat16)
    new_probs = (new_exp / total).astype(jnp.bfloat16)
    attended = jnp.einsum("rqj,rjd->rqd", old_probs, value_old, preferred_element_type=jnp.float32)
    attended = attended + jnp.einsum(
        "rqt,rtd->rqd", new_probs, value_rows, preferred_element_type=jnp.float32
    )
    attended = attended.astype(jnp.bfloat16).reshape(row_count, step_count, heads_here, head_size)
    attended = attended.transpose(1, 0, 2, 3).reshape(token_count, heads_here * head_size)
    out_part = lax.all_to_all(o_weight, "tp", split_axis=1, concat_axis=0, tiled=True)
    projected = lax.dot_general(
        attended,
        lax.all_gather(out_part, "rep", axis=0, tiled=True),
        (((1,), (1,)), ((), ())),
        preferred_element_type=jnp.float32,
    )
    projected = projected.reshape(step_count, row_count, rep_count, tp_count, o_weight.shape[0])
    head_total = (
        lax.psum_scatter(projected.astype(jnp.bfloat16), "tp", scatter_dimension=3, tiled=True)
        .astype(jnp.float32)
        .reshape(step_count, row_count, share)
    )
    residual = lax.dynamic_slice_in_dim(hidden_f, tp_index * share, share, 2)
    active = jnp.arange(step_count, dtype=jnp.int32)[:, None] <= finish[None, :]
    decoded = jnp.where(active[:, :, None], head_total + residual, 0.0).astype(jnp.bfloat16)
    chosen = jnp.arange(step_count, dtype=jnp.int32)[:, None] == finish[None, :]
    at_finish = jnp.sum(jnp.where(chosen[:, :, None], decoded.astype(jnp.float32), 0.0), axis=0)
    is_returned = finish < step_count
    owner_flat = owner[:, 0]
    row_ids = jnp.arange(row_count)
    same = (
        (owner_flat[:, None] == owner_flat[None, :])
        & is_returned[None, :]
        & (row_ids[None, :] < row_ids[:, None])
    )
    rank = jnp.sum(same.astype(jnp.int32), axis=1)
    device_count = rep_count * tp_count
    capacity = max(2, 2 * row_count // device_count)
    slot = jnp.where(is_returned, owner_flat * capacity + rank, -1)
    one_hot = (jnp.arange(device_count * capacity)[:, None] == slot[None, :]).astype(jnp.bfloat16)
    outgoing = jnp.dot(
        one_hot, at_finish.astype(jnp.bfloat16), preferred_element_type=jnp.float32
    ).astype(jnp.bfloat16)
    arrived = lax.all_to_all(
        outgoing.reshape(device_count, capacity, share),
        ("rep", "tp"),
        split_axis=0,
        concat_axis=2,
        tiled=True,
    )
    returned = arrived.reshape(capacity * rep_count, model_width)
    return (decoded, returned)


def solution(mesh):
    placed = (
        P(None, "rep", None),
        P(),
        P(("rep", "tp"), None),
        P(("rep", "tp"), None),
        P(("rep", "tp"), None),
        P(("tp", "rep"), None),
        P("rep", "tp", None, None),
        P("rep", "tp", None, None),
        P("rep"),
        P("rep"),
        P("rep", None),
    )
    return jax.shard_map(
        per_device,
        mesh=mesh,
        in_specs=placed,
        out_specs=(P(None, "rep", "tp"), P(("rep", "tp"), None)),
        check_vma=False,
    )
```

profile of v0, /device:TPU:1, one launch (start us, length us, event | category | flops | bytes accessed | tf_op | source)
XLA Modules:
  0.0 517.1 jit_solution(6755973237441349800)
XLA Ops:
  7.2 1.0 copy.84
  8.2 0.9 copy.85
  9.2 0.3 copy.68
  9.5 0.4 broadcast_in_dim.52
  9.9 0.3 all_to_all.57
  10.2 20.7 %all_to_all.72 = bf16[64,16,256]{2,0,1:T(8,128)(2,1)} all-to-all(bf16[64,16,256]{2,0,1:T(8,128)(2,1)S(1)} %all_to_all.57), channel_id=1, replica_groups=mesh['rep'=8,'tp'=16] {'tp'}, dimensions={1} | all-to-all | bytes 1048576 | tf_op jit(solution)/shard_map/all_to_all | solution.py:53
  31.0 1.3 copy.91
  32.3 60.6 %all_to_all.73 = bf16[64,16,512]{2,0,1:T(8,128)(2,1)} all-to-all(bf16[64,16,512]{2,0,1:T(8,128)(2,1)S(1)} %bitcast.108), channel_id=1, replica_groups=mesh['rep'=8,'tp'=16] {'tp'}, dimensions={1} | all-to-all | bytes 2097152 | tf_op jit(solution)/shard_map/all_to_all | solution.py:52
  93.1 99.9 %all_to_all.74 = bf16[64,16,512]{2,0,1:T(8,128)(2,1)} all-to-all(bf16[64,16,512]{2,0,1:T(8,128)(2,1)S(1)} %bitcast.109), channel_id=1, replica_groups=mesh['rep'=8,'tp'=16] {'tp'}, dimensions={1} | all-to-all | bytes 2097152 | tf_op jit(solution)/shard_map/all_to_all | solution.py:112
  193.2 5.1 multiply_reduce_fusion
  198.4 10.1 %multiply_convert_fusion = bf16[4,128,8192]{2,1,0:T(8,128)(2,1)} fusion(f32[8192]{0:T(1024)S(1)} %convert_element_type.51, f32[4,128]{1,0:T(4,128)S(1)} %add_rsqrt_fusion, bf16[4,128,8192]{2,1,0:T(8,128)(2,1)} %param.11), kind=kLoop, calls=%fused_computation | loop fusion | flops 16777216 | bytes 16812032 | tf_op jit(solution)/shard_map/convert_element_type | solution.py:57
  208.5 7.1 %fusion.29 = f32[512,256]{0,1:T(8,128)S(1)} fusion(bf16[512,8192]{1,0:T(8,128)(2,1)} %bitcast.103, bf16[8192,256]{1,0:T(8,128)(2,1)} %all-gather.6.cloned.1.call-done), kind=kOutput, calls=%fused_computation.72 | convolution fusion | flops 2147483648 | bytes 13107200 | tf_op jit(solution)/shard_map/dot_general | solution.py:67
  215.6 0.6 subtract_convert_fusion.1
  216.8 12.1 %copy.66 = bf16[512,8192]{1,0:T(8,128)(2,1)} copy(bf16[512,8192]{0,1:T(8,128)(2,1)} %bitcast.102) | data formatting | bytes 16777216 | tf_op jit(solution)/shard_map/dot_general | solution.py:66
  228.8 9.6 %fusion.28 = f32[512,4,128]{0,2,1:T(8,128)S(1)} fusion(bf16[512,8192,1]{1,0,2:T(8,128)(2,1)} %bitcast.104, bf16[4,128,8192]{2,1,0:T(8,128)(2,1)} %bitcast.105), kind=kOutput, calls=%fused_computation.71 | convolution fusion | flops 4294967296 | bytes 17825792 | tf_op jit(solution)/shard_map/dot_general | solution.py:66
  238.7 0.3 maximum_bitcast_fusion
  239.1 0.6 copy.67
  239.7 0.5 fusion.27
  240.1 6.5 %fusion.4 = (f32[128,16]{1,0:T(8,128)S(1)}, f32[128,16,192]{2,1,0:T(8,128)S(1)}) fusion(pred[128,192]{1,0:T(8,128)(4,1)S(1)} %iota_compare_fusion.1, bf16[128,16,128]{2,1,0:T(8,128)(2,1)S(1)} %bitcast.111, bf16[128,1,192,128]{3,2,1,0:T(8,128)(2,1)} %param.17), kind=kOutput, calls=%fused_computation.10 | convolution fusion | flops 101840896 | bytes 8421376 | tf_op jit(solution)/shard_map/rqd,rjd->rqj/dot_general | solution.py:88
  247.0 1.1 fusion.5
  248.1 1.8 fusion
  249.9 0.4 fusion.6
  250.5 31.2 %all-gather.8.cloned.1.call-done = bf16[8192,512]{1,0:T(8,128)(2,1)} async-done(((bf16[1024,512]{1,0:T(8,128)(2,1)}), bf16[8192,512]{1,0:T(8,128)(2,1)}) %all-gather.8.cloned.1.call-update) | async-done | bytes 8388624 | tf_op jit(solution)/shard_map/all_gather | solution.py:115
  281.7 10.2 %convolution_convert_fusion = bf16[4,128,8,16,64]{1,4,3,2,0:T(8,128)(2,1)} fusion(bf16[8,16,64,512,1]{3,2,1,0,4:T(8,128)(2,1)} %bitcast.124, bf16[4,128,512,1,1]{2,0,1,4,3:T(4,128)(2,1)S(1)} %bitcast.116), kind=kOutput, calls=%fused_computation.2 | convolution fusion | flops 4299161600 | bytes 17301504 | tf_op jit(solution)/shard_map/dot_general | solution.py:113
  292.0 11.5 %convert_element_type.50 = f32[4,128,8192]{2,1,0:T(8,128)} convert(bf16[4,128,8192]{2,1,0:T(8,128)(2,1)} %param.11) | non-fusion elementwise | flops 4194304 | bytes 25165824 | tf_op jit(solution)/shard_map/convert_element_type | solution.py:55
  303.5 0.6 dynamic-slice
  304.3 182.0 %all-reduce.3.cloned.1.call-done = bf16[4,128,8,16,64]{1,4,3,2,0:T(8,128)(2,1)} async-done(((bf16[4,128,8,16,64]{1,4,3,2,0:T(8,128)(2,1)}), bf16[4,128,8,16,64]{1,4,3,2,0:T(8,128)(2,1)}) %all-reduce.3.cloned.1.call-update) | async-done | bytes 8388624
  486.3 1.7 constant_dynamic-slice_fusion
  488.1 0.3 copy.74
  488.5 2.2 select_reduce_fusion
  491.1 18.6 %all_to_all.75 = bf16[128,2,512]{2,1,0:T(2,128)(2,1)S(1)} all-to-all(bf16[128,2,512]{2,1,0:T(2,128)(2,1)S(1)} %reshape.268), channel_id=1, replica_groups=mesh['rep'=8,'tp'=16] {'rep','tp'}, dimensions={0} | all-to-all | bytes 524288 | tf_op jit(solution)/shard_map/all_to_all | solution.py:146
  509.7 0.8 reshape.269
  (59 shorter events, 2.5 us)
Async XLA Ops:
  7.2 85.8 %copy-start = (bf16[64,8192]{1,0:T(8,128)(2,1)S(1)}, bf16[64,8192]{1,0:T(8,128)(2,1)}, u32[]{:S(2)}) copy-start(bf16[64,8192]{1,0:T(8,128)(2,1)} %param.16) | copy-start | bytes 3145732
  7.2 201.3 %all-gather.6.cloned.1.call-start = ((), (), s32[]{:S(2)}) async-start(), calls=%async_computation.5 | async-start | bytes 4718592 | tf_op jit(solution)/shard_map/all_gather | solution.py:64
  10.2 182.9 %copy-start.1 = (bf16[8192]{0:T(1024)(128)(2,1)S(1)}, bf16[8192]{0:T(1024)(128)(2,1)}, u32[]{:S(2)}) copy-start(bf16[8192]{0:T(1024)(128)(2,1)} %param.12) | copy-start | bytes 49156
  30.9 185.8 %all-gather.4.cloned.1.call-start = ((), (), s32[]{:S(2)}) async-start(), calls=%async_computation.4 | async-start | bytes 9437184 | tf_op jit(solution)/shard_map/all_gather | solution.py:63
  92.9 188.8 %all-gather.8.cloned.1.call-start = ((), (), s32[]{:S(2)}) async-start(), calls=%async_computation.6 | async-start | bytes 9437184 | tf_op jit(solution)/shard_map/all_gather | solution.py:115
  93.1 105.2 %copy-start.3 = (s32[128]{0:T(128)S(1)}, s32[128]{0:T(128)}, u32[]{:S(2)}) copy-start(s32[128]{0:T(128)} %param.19) | copy-start | bytes 1540
  193.1 293.2 %all-reduce.3.cloned.1.call-start = ((), (), s32[]{:S(2)}) async-start(), calls=%async_computation.7 | async-start | bytes 16777216
  239.6 8.5 %slice-start = ((s8[6291456]{0:T(1024)(128)(4,1)}), s8[4194304]{0:T(1024)(128)(4,1)S(1)}, s32[]{:S(2)}) async-start(s8[6291456]{0:T(1024)(128)(4,1)} %bitcast.125), calls=%async_computation.8 | async-start | bytes 8388608
  240.1 8.0 %slice-start.1 = ((s8[6291456]{0:T(1024)(128)(4,1)}), s8[2097152]{0:T(1024)(128)(4,1)S(1)}, s32[]{:S(2)}) async-start(s8[6291456]{0:T(1024)(128)(4,1)} %bitcast.125), calls=%async_computation.9 | async-start | bytes 4194304
  291.9 11.6 %copy-start.5 = (u32[128]{0:T(128)S(1)}, u32[128]{0:T(128)}, u32[]{:S(2)}) copy-start(u32[128]{0:T(128)} %constant.58) | copy-start | bytes 1540
  292.0 12.2 %copy-start.4 = (s32[128]{0:T(128)S(1)}, s32[128]{0:T(128)}, u32[]{:S(2)}) copy-start(s32[128]{0:T(128)} %param.20) | copy-start | bytes 1540
  292.0 12.2 %copy-start.2 = (s32[128,1]{0,1:T(1,128)S(1)}, s32[128,1]{0,1:T(1,128)}, u32[]{:S(2)}) copy-start(s32[128,1]{0,1:T(1,128)} %param.21) | copy-start | bytes 1540
Sparse Core Ops, SparseCore 0:
  31.0 49.7 all-gather.5
  93.0 88.4 all-gather.3
  193.2 88.4 all-gather.7
  292.1 194.1 all-reduce.2
where the time goes:
time: 518 us; the launch traced here: 517 us
  waiting for transfers between devices  213 us (41%)
  blocking collectives  200 us (39%)
  matrix products  36.2 us (7%)
  other arithmetic  31.9 us (6%)
  local copies, waits for them, and re-layouts  21.5 us (4%)
  between operations  14.2 us (3%)
    unnamed x5, waiting for transfers between devices  182 us
    all_to_all x1, blocking collectives, per_device(): lax.all_to_all(o_weight, 'tp', split_axis=1, concat_axis=0, tiled=True)  99.9 us
    all_to_all x1, blocking collectives, per_device(): lax.all_to_all(q_weight, 'tp', split_axis=1, concat_axis=0, tiled=True)  60.6 us
    all_gather x1, waiting for transfers between devices, per_device(): lax.all_gather(out_part, 'rep', axis=0, tiled=True)  31.2 us
    all_to_all x1, blocking collectives, per_device(): lax.all_to_all(kv_spread, 'tp', split_axis=1, concat_axis=0, tiled=True)  20.7 us
    all_to_all x1, blocking collectives, per_device(): lax.all_to_all(outgoing.reshape(device_count, capacity, share), ('rep', '...  18.6 us
    dot_general x1, local copies, waits for them, and re-layouts, per_device(): jnp.dot(normed_flat, query_full, preferred_element_type=jnp.float32)  12.1 us
    convert_element_type x1, other arithmetic, per_device(): hidden_f = hidden.astype(jnp.float32)  11.5 us
  transfers between devices with their start and end apart: 4, of which 2 were waited for; matrix products, arithmetic and copies ran while one was open for 14% of the time, Pallas kernels for 0%

commit v1 on v0

--- a/solution.py
+++ b/solution.py
@@ -109,19 +109,11 @@
     )
     attended = attended.astype(jnp.bfloat16).reshape(row_count, step_count, heads_here, head_size)
     attended = attended.transpose(1, 0, 2, 3).reshape(token_count, heads_here * head_size)
-    out_part = lax.all_to_all(o_weight, "tp", split_axis=1, concat_axis=0, tiled=True)
-    projected = lax.dot_general(
-        attended,
-        lax.all_gather(out_part, "rep", axis=0, tiled=True),
-        (((1,), (1,)), ((), ())),
-        preferred_element_type=jnp.float32,
-    )
-    projected = projected.reshape(step_count, row_count, rep_count, tp_count, o_weight.shape[0])
-    head_total = (
-        lax.psum_scatter(projected.astype(jnp.bfloat16), "tp", scatter_dimension=3, tiled=True)
-        .astype(jnp.float32)
-        .reshape(step_count, row_count, share)
-    )
+    attended_full = lax.all_gather(attended, "tp", axis=1, tiled=True)
+    out_rows = lax.all_gather(o_weight, "rep", axis=0, tiled=True)
+    head_total = lax.dot_general(
+        attended_full, out_rows, (((1,), (1,)), ((), ())), preferred_element_type=jnp.float32
+    ).reshape(step_count, row_count, share)
     residual = lax.dynamic_slice_in_dim(hidden_f, tp_index * share, share, 2)
     active = jnp.arange(step_count, dtype=jnp.int32)[:, None] <= finish[None, :]
     decoded = jnp.where(active[:, :, None], head_total + residual, 0.0).astype(jnp.bfloat16)

time: 518 us -> 390 us (0.75)
  blocking collectives: 200 us -> 97.5 us
  waiting for transfers between devices: 213 us -> 191 us
    unnamed x5 -> x4, waiting for transfers between devices: 182 us -> 0.73 us
    all_to_all x1 -> x0, blocking collectives: 99.9 us -> none  [per_device(): lax.all_to_all(o_weight, 'tp', split_axis=1, concat_axis=0, tiled=True)]
    all_gather x1 -> x2, waiting for transfers between devices: 31.2 us -> 126 us  [the longest x1 79.3 us: per_device(): attended_full = lax.all_gather(attended, 'tp', axis=1, tiled=True)]
    all_gather x1, waiting for transfers between devices: 0.02 us -> 64.4 us  [per_device(): lax.all_gather(query_part, 'rep', axis=0, tiled=True)]
  transfers between devices with their start and end apart: 4 -> 4, of which waited for: 2 -> 3; matrix products, arithmetic and copies ran while one was open for 14% -> 18% of each run, Pallas kernels for 0% -> 0%
where the time goes in v1:
time: 390 us; the launch traced here: 389 us
  waiting for transfers between devices  191 us (49%)
  blocking collectives  97.5 us (25%)
  matrix products  35.4 us (9%)
  other arithmetic  31.5 us (8%)
  local copies, waits for them, and re-layouts  19.3 us (5%)
  between operations  14.1 us (4%)
    all_gather x1, waiting for transfers between devices, per_device(): attended_full = lax.all_gather(attended, 'tp', axis=1, tiled=True)  79.3 us
    all_gather x1, waiting for transfers between devices, per_device(): lax.all_gather(query_part, 'rep', axis=0, tiled=True)  64.4 us
    all_to_all x1, blocking collectives, per_device(): lax.all_to_all(q_weight, 'tp', split_axis=1, concat_axis=0, tiled=True)  60.6 us
    all_gather x1, waiting for transfers between devices, per_device(): out_rows = lax.all_gather(o_weight, 'rep', axis=0, tiled=True)  46.5 us
    all_to_all x1, blocking collectives, per_device(): lax.all_to_all(kv_spread, 'tp', split_axis=1, concat_axis=0, tiled=True)  20.7 us
    all_to_all x1, blocking collectives, per_device(): lax.all_to_all(outgoing.reshape(device_count, capacity, share), ('rep', '...  16.2 us
    dot_general x1, local copies, waits for them, and re-layouts, per_device(): jnp.dot(normed_flat, query_full, preferred_element_type=jnp.float32)  11.8 us
    convert_element_type x1, other arithmetic, per_device(): hidden_f = hidden.astype(jnp.float32)  11.4 us
  transfers between devices with their start and end apart: 4, of which 3 were waited for; matrix products, arithmetic and copies ran while one was open for 18% of the time, Pallas kernels for 0%

profile of v1, /device:TPU:1, one launch (start us, length us, event | category | flops | bytes accessed | tf_op | source)
XLA Modules:
  0.0 388.9 jit_solution(2181237983379067531)
XLA Ops:
  7.2 0.9 copy.57
  8.1 0.9 copy.56
  9.1 0.3 copy.49
  9.4 0.4 broadcast_in_dim.52
  9.8 0.3 all_to_all.43
  10.1 20.7 %all_to_all.53 = bf16[64,16,256]{2,0,1:T(8,128)(2,1)} all-to-all(bf16[64,16,256]{2,0,1:T(8,128)(2,1)S(1)} %all_to_all.43), channel_id=1, replica_groups=mesh['rep'=8,'tp'=16] {'tp'}, dimensions={1} | all-to-all | bytes 1048576 | tf_op jit(solution)/shard_map/all_to_all | solution.py:53
  30.9 1.3 copy.61
  32.2 60.6 %all_to_all.54 = bf16[64,16,512]{2,0,1:T(8,128)(2,1)} all-to-all(bf16[64,16,512]{2,0,1:T(8,128)(2,1)S(1)} %bitcast.88), channel_id=1, replica_groups=mesh['rep'=8,'tp'=16] {'tp'}, dimensions={1} | all-to-all | bytes 2097152 | tf_op jit(solution)/shard_map/all_to_all | solution.py:52
  92.9 0.7 all-gather.11.cloned.1.call-update
  93.7 5.1 %multiply_reduce_fusion = f32[4,128]{1,0:T(4,128)S(1)} fusion(bf16[4,128,8192]{2,1,0:T(8,128)(2,1)} %param.11), kind=kLoop, calls=%fused_computation.1 | loop fusion | flops 12582400 | bytes 8390656 | tf_op jit(solution)/shard_map/reduce_sum | solution.py:56
  98.9 9.9 %multiply_convert_fusion = bf16[4,128,8192]{2,1,0:T(8,128)(2,1)} fusion(f32[8192]{0:T(1024)S(1)} %convert_element_type.47, f32[4,128]{1,0:T(4,128)S(1)} %add_rsqrt_fusion, bf16[4,128,8192]{2,1,0:T(8,128)(2,1)} %param.11), kind=kLoop, calls=%fused_computation | loop fusion | flops 16777216 | bytes 16812032 | tf_op jit(solution)/shard_map/convert_element_type | solution.py:57
  108.8 7.1 %fusion.28 = f32[512,256]{0,1:T(8,128)S(1)} fusion(bf16[512,8192]{1,0:T(8,128)(2,1)} %bitcast.84, bf16[8192,256]{1,0:T(8,128)(2,1)} %all-gather.7.cloned.1.call-done), kind=kOutput, calls=%fused_computation.68 | convolution fusion | flops 2147483648 | bytes 13107200 | tf_op jit(solution)/shard_map/dot_general | solution.py:67
  115.9 0.6 subtract_convert_fusion.1
  117.1 64.4 %all-gather.5.cloned.1.call-done = bf16[8192,512]{1,0:T(8,128)(2,1)} async-done(((bf16[1024,512]{1,0:T(8,128)(2,1)}), bf16[8192,512]{1,0:T(8,128)(2,1)}) %all-gather.5.cloned.1.call-update) | async-done | bytes 8388624 | tf_op jit(solution)/shard_map/all_gather | solution.py:63
  181.5 11.8 %copy.47 = bf16[512,8192]{1,0:T(8,128)(2,1)} copy(bf16[512,8192]{0,1:T(8,128)(2,1)} %bitcast.83) | data formatting | bytes 16777216 | tf_op jit(solution)/shard_map/dot_general | solution.py:66
  193.3 9.4 %fusion.27 = f32[512,4,128]{0,2,1:T(8,128)S(1)} fusion(bf16[512,8192,1]{1,0,2:T(8,128)(2,1)} %bitcast.85, bf16[4,128,8192]{2,1,0:T(8,128)(2,1)} %bitcast.86), kind=kOutput, calls=%fused_computation.67 | convolution fusion | flops 4294967296 | bytes 17825792 | tf_op jit(solution)/shard_map/dot_general | solution.py:66
  203.0 0.3 maximum_bitcast_fusion
  203.4 0.6 copy.48
  204.0 0.5 fusion.26
  204.5 6.5 %fusion.4 = (f32[128,16]{1,0:T(8,128)S(1)}, f32[128,16,192]{2,1,0:T(8,128)S(1)}) fusion(pred[128,192]{1,0:T(8,128)(4,1)S(1)} %iota_compare_fusion.1, bf16[128,16,128]{2,1,0:T(8,128)(2,1)S(1)} %bitcast.90, bf16[128,1,192,128]{3,2,1,0:T(8,128)(2,1)} %param.17), kind=kOutput, calls=%fused_computation.9 | convolution fusion | flops 101840896 | bytes 8421376 | tf_op jit(solution)/shard_map/rqd,rjd->rqj/dot_general | solution.py:88
  211.0 0.2 fusion.13
  211.3 1.1 fusion.5
  212.4 1.8 fusion
  214.3 0.4 fusion.6
  214.8 0.9 copy.62
  215.8 11.4 %convert_element_type.46 = f32[4,128,8192]{2,1,0:T(8,128)} convert(bf16[4,128,8192]{2,1,0:T(8,128)(2,1)} %param.11) | non-fusion elementwise | flops 4194304 | bytes 25165824 | tf_op jit(solution)/shard_map/convert_element_type | solution.py:55
  227.4 46.5 %all-gather.11.cloned.1.call-done = bf16[512,8192]{1,0:T(8,128)(2,1)} async-done(((bf16[64,8192]{1,0:T(8,128)(2,1)}), bf16[512,8192]{1,0:T(8,128)(2,1)}) %all-gather.11.cloned.1.call-update) | async-done | bytes 8388624 | tf_op jit(solution)/shard_map/all_gather | solution.py:113
  273.8 79.3 %all-gather.9.cloned.1.call-done = bf16[512,8192]{1,0:T(8,128)(2,1)} async-done(((bf16[512,512]{1,0:T(8,128)(2,1)}), bf16[512,8192]{1,0:T(8,128)(2,1)}) %all-gather.9.cloned.1.call-update) | async-done | bytes 8388624 | tf_op jit(solution)/shard_map/all_gather | solution.py:112
  353.1 9.5 %fusion.29 = f32[512,512]{1,0:T(8,128)S(1)} fusion(bf16[512,8192]{1,0:T(8,128)(2,1)} %all-gather.9.cloned.1.call-done, bf16[512,8192]{1,0:T(8,128)(2,1)} %all-gather.11.cloned.1.call-done), kind=kOutput, calls=%fused_computation.69 | convolution fusion | flops 4294967296 | bytes 17825792 | tf_op jit(solution)/shard_map/dot_general | solution.py:114
  362.6 2.3 select_reduce_fusion
  365.3 16.2 %all_to_all.55 = bf16[128,2,512]{2,1,0:T(2,128)(2,1)S(1)} all-to-all(bf16[128,2,512]{2,1,0:T(2,128)(2,1)S(1)} %reshape.260), channel_id=1, replica_groups=mesh['rep'=8,'tp'=16] {'rep','tp'}, dimensions={0} | all-to-all | bytes 524288 | tf_op jit(solution)/shard_map/all_to_all | solution.py:138
  381.5 0.8 reshape.261
  (50 shorter events, 2.0 us)
Async XLA Ops:
  7.2 86.5 %copy-start = (bf16[8192]{0:T(1024)(128)(2,1)S(1)}, bf16[8192]{0:T(1024)(128)(2,1)}, u32[]{:S(2)}) copy-start(bf16[8192]{0:T(1024)(128)(2,1)} %param.12) | copy-start | bytes 49156
  7.2 101.7 %all-gather.7.cloned.1.call-start = ((), (), s32[]{:S(2)}) async-start(), calls=%async_computation.4 | async-start | bytes 4718592 | tf_op jit(solution)/shard_map/all_gather | solution.py:64
  30.8 150.6 %all-gather.5.cloned.1.call-start = ((), (), s32[]{:S(2)}) async-start(), calls=%async_computation.3 | async-start | bytes 9437184 | tf_op jit(solution)/shard_map/all_gather | solution.py:63
  32.2 66.6 %copy-start.2 = (s32[128]{0:T(128)S(1)}, s32[128]{0:T(128)}, u32[]{:S(2)}) copy-start(s32[128]{0:T(128)} %param.19) | copy-start | bytes 1540
  92.9 181.0 %all-gather.11.cloned.1.call-start = ((), (), s32[]{:S(2)}) async-start(), calls=%async_computation.6 | async-start | bytes 9437184 | tf_op jit(solution)/shard_map/all_gather | solution.py:113
  93.6 259.5 %all-gather.9.cloned.1.call-start = ((), (), s32[]{:S(2)}) async-start(), calls=%async_computation.5 | async-start | bytes 8912896 | tf_op jit(solution)/shard_map/all_gather | solution.py:112
  204.0 8.5 %slice-start = ((s8[6291456]{0:T(1024)(128)(4,1)}), s8[4194304]{0:T(1024)(128)(4,1)S(1)}, s32[]{:S(2)}) async-start(s8[6291456]{0:T(1024)(128)(4,1)} %bitcast.104), calls=%async_computation.7 | async-start | bytes 8388608
  204.4 8.0 %slice-start.1 = ((s8[6291456]{0:T(1024)(128)(4,1)}), s8[2097152]{0:T(1024)(128)(4,1)S(1)}, s32[]{:S(2)}) async-start(s8[6291456]{0:T(1024)(128)(4,1)} %bitcast.104), calls=%async_computation.8 | async-start | bytes 4194304
  215.7 11.4 %copy-start.3 = (s32[128]{0:T(128)S(1)}, s32[128]{0:T(128)}, u32[]{:S(2)}) copy-start(s32[128]{0:T(128)} %param.20) | copy-start | bytes 1540
  215.7 11.4 %copy-start.1 = (s32[128,1]{0,1:T(1,128)S(1)}, s32[128,1]{0,1:T(1,128)}, u32[]{:S(2)}) copy-start(s32[128,1]{0,1:T(1,128)} %param.21) | copy-start | bytes 1540
Sparse Core Ops, SparseCore 0:
  30.9 49.7 all-gather.6
  93.0 88.4 all-gather.4
  183.1 90.6 all-gather.10
  276.6 76.4 all-gather.8

commit v2 on v1

v2 whole, which is shorter than its diff:
```python
import jax
import jax.numpy as jnp
from jax import lax
from jax.experimental import pallas as pl
from jax.experimental.pallas import tpu as pltpu
from jax.sharding import PartitionSpec as P

MESH = pl.DeviceIdType.MESH
KV = 8
STEPS = 4
ROWS = 128
HD = 128
CACHE = 192
KEYS = CACHE + 16
D = 8192
REP = 8
TP = 16
QC = 512
WC = QC + HD
SHARD = 64
BLOCK = TP * SHARD
TOKENS = STEPS * ROWS
CHUNKS = 4
CROWS = ROWS // CHUNKS
CTOK = CROWS * STEPS
EPS = 1e-05

QKV_CUT = 576
OUT_CUT = 5120


def kernel(
    hidden,
    gain,
    q_weight,
    k_weight,
    v_weight,
    o_weight,
    key_cache,
    value_cache,
    lens,
    finish,
    cosine,
    sine,
    one_hot,
    decoded,
    returned,
    staged,
    normed,
    weights,
    out_rows,
    keys,
    values,
    acc,
    queries,
    pair,
    attn_rows,
    gathered,
    out_acc,
    residual,
    at_finish,
    outgoing,
    stage_one,
    spread,
    stage_two,
    arrived,
    load_sem,
    local_sem,
    a2a_send,
    a2a_recv,
    qkv_send,
    qkv_recv,
    out_send,
    out_recv,
    pair_send,
    pair_recv,
    attn_send,
    attn_recv,
    one_send,
    one_recv,
    two_send,
    two_recv,
):
    rep = lax.axis_index("rep")
    tp = lax.axis_index("tp")
    y, x = rep // 4, rep % 4
    across = (1 - y) * 4
    mine = y * 4
    east, west, far = (x + 1) % 4, (x + 3) % 4, (x + 2) % 4
    rep_east, rep_west, rep_y = mine + east, mine + west, across + x
    z, low = tp // 4, tp % 4
    core_peer = tp + 1 - 2 * (tp % 2)
    hi_peer = tp + 2 - 4 * ((tp // 2) % 2)
    pending = []

    def send(src, dst, sends, recvs, k, to):
        copy = pltpu.make_async_remote_copy(
            src_ref=src,
            dst_ref=dst,
            send_sem=sends.at[k],
            recv_sem=recvs.at[k],
            device_id=to,
            device_id_type=MESH,
        )
        copy.start()
        pending.append(copy)

    def receive(region, sends, recvs, k):
        pltpu.make_async_remote_copy(
            src_ref=region,
            dst_ref=region,
            send_sem=sends.at[k],
            recv_sem=recvs.at[k],
            device_id=(rep, core_peer),
            device_id_type=MESH,
        ).wait_recv()

    barrier = pltpu.get_barrier_semaphore()
    for d in range(1, TP):
        pl.semaphore_signal(
            barrier, inc=1, device_id=(rep, (tp + d) % TP), device_id_type=MESH
        )
    for d in range(1, REP):
        pl.semaphore_signal(
            barrier, inc=1, device_id=((rep + d) % REP, tp), device_id_type=MESH
        )
    key_load = pltpu.make_async_copy(
        key_cache.at[:, 0], keys.at[:, pl.ds(0, CACHE), :], local_sem.at[0]
    )
    value_load = pltpu.make_async_copy(
        value_cache.at[:, 0], values.at[:, pl.ds(0, CACHE), :], local_sem.at[1]
    )
    my_cols = pl.ds(pl.multiple_of(tp * QC, QC), QC)
    residual_load = pltpu.make_async_copy(
        hidden.at[:, :, my_cols], residual, local_sem.at[2]
    )
    my_rows = pl.ds(pl.multiple_of(tp * SHARD, SHARD), SHARD)
    q_load = pltpu.make_async_copy(
        q_weight.at[:, my_cols], weights.at[rep, my_rows, pl.ds(0, QC)], local_sem.at[3]
    )
    kv_cols = pl.ds(pl.multiple_of((tp // 2) * HD, HD), HD)
    my_kv = weights.at[rep, my_rows, pl.ds(QC, HD)]
    k_load = pltpu.make_async_copy(k_weight.at[:, kv_cols], my_kv, local_sem.at[4])
    v_load = pltpu.make_async_copy(v_weight.at[:, kv_cols], my_kv, local_sem.at[4])

    def out_block(r, part):
        start, size = {
            "A": (0, OUT_CUT),
            "A0": (0, OUT_CUT // 2),
            "A1": (OUT_CUT // 2, OUT_CUT // 2),
            "B": (OUT_CUT, D - OUT_CUT),
            "B0": (OUT_CUT, (D - OUT_CUT) // 2),
            "B1": (OUT_CUT + (D - OUT_CUT) // 2, (D - OUT_CUT) // 2),
            "all": (0, D),
        }[part]
        return out_rows.at[
            pl.ds(pl.multiple_of(r * SHARD, SHARD), SHARD), pl.ds(start, size)
        ]

    def qkv_block(r, part):
        start, size = {
            "A": (0, QKV_CUT),
            "A0": (0, QKV_CUT // 2),
            "A1": (QKV_CUT // 2, QKV_CUT // 2),
            "B": (QKV_CUT, BLOCK - QKV_CUT),
            "B0": (QKV_CUT, (BLOCK - QKV_CUT) // 2),
            "B1": (QKV_CUT + (BLOCK - QKV_CUT) // 2, (BLOCK - QKV_CUT) // 2),
        }[part]
        return weights.at[r, pl.ds(start, size), :]

    out_load = pltpu.make_async_copy(o_weight, out_block(rep, "all"), local_sem.at[5])
    q_load.start()
    pl.when(tp % 2 == 0)(k_load.start)
    pl.when(tp % 2 == 1)(v_load.start)
    out_load.start()

    def hidden_load(step, slot):
        return pltpu.make_async_copy(
            hidden.at[step // CHUNKS, pl.ds(pl.multiple_of((step % CHUNKS) * CROWS, CROWS), CROWS), :],
            staged.at[slot],
            load_sem.at[slot],
        )

    hidden_load(0, 0).start()
    pl.semaphore_wait(barrier, TP - 1 + REP - 1)

    for d in range(1, TP):
        to = (tp + d) % TP
        there = (rep, to)
        send(
            q_weight.at[:, pl.ds(pl.multiple_of(to * QC, QC), QC)],
            weights.at[rep, my_rows, pl.ds(0, QC)],
            a2a_send,
            a2a_recv,
            d,
            there,
        )
        cols = pl.ds(pl.multiple_of((to // 2) * HD, HD), HD)

        def kv_copy(source, cols=cols, d=d, there=there):
            return pltpu.make_async_remote_copy(
                src_ref=source.at[:, cols],
                dst_ref=weights.at[rep, my_rows, pl.ds(QC, HD)],
                send_sem=a2a_send.at[TP + d],
                recv_sem=a2a_recv.at[TP + d],
                device_id=there,
                device_id_type=MESH,
            )

        from_k, from_v = kv_copy(k_weight), kv_copy(v_weight)
        pl.when(to % 2 == 0)(from_k.start)
        pl.when(to % 2 == 1)(from_v.start)
        pending.append(from_k)

    east_dev, west_dev, y_dev = (rep_east, tp), (rep_west, tp), (rep_y, tp)

    def ring(block, sends, recvs):
        def go(k, r, part, to, src=None):
            send(src if src is not None else block(r, part), block(r, part), sends, recvs, k, to)

        def got(k, r, part):
            receive(block(r, part), sends, recvs, k)

        return go, got

    o_go, o_got = ring(out_block, out_send, out_recv)
    w_go, w_got = ring(qkv_block, qkv_send, qkv_recv)

    o_a = o_weight.at[:, pl.ds(0, OUT_CUT)]
    o_b = o_weight.at[:, pl.ds(OUT_CUT, D - OUT_CUT)]
    o_go(9, rep, "B", east_dev, o_b)
    o_go(10, rep, "B", west_dev, o_b)
    o_go(0, rep, "A", y_dev, o_a)
    o_go(1, rep, "A", east_dev, o_a)
    o_go(2, rep, "A", west_dev, o_a)

    key_load.start()
    value_load.start()
    residual_load.start()

    def norm_step(step, carry):
        slot = step % 2
        hidden_load(step, slot).wait()

        @pl.when(step + 1 < STEPS * CHUNKS)
        def _():
            hidden_load(step + 1, 1 - slot).start()

        values_f = staged[slot].astype(jnp.float32)
        mean = jnp.mean(values_f * values_f, axis=-1, keepdims=True)
        scale = lax.rsqrt(mean + EPS)
        out = (values_f * scale * gain[...].astype(jnp.float32)).astype(jnp.bfloat16)
        rows = pl.ds(pl.multiple_of(step * CROWS, CROWS), CROWS)
        for r in range(REP):
            normed[r, rows, :] = out[:, r * BLOCK : (r + 1) * BLOCK]
        return carry

    lax.fori_loop(0, STEPS * CHUNKS, norm_step, 0)

    q_load.wait()
    k_load.wait()
    for d in range(1, TP):
        source = (tp + TP - d) % TP
        rows = pl.ds(pl.multiple_of(source * SHARD, SHARD), SHARD)
        receive(weights.at[rep, rows, pl.ds(0, QC)], a2a_send, a2a_recv, d)
        receive(weights.at[rep, rows, pl.ds(QC, HD)], a2a_send, a2a_recv, TP + d)

    def project(r, first=False):
        def tile(m, carry):
            rows = pl.ds(pl.multiple_of(m * 256, 256), 256)
            part = jnp.dot(normed[r, rows, :], weights[r], preferred_element_type=jnp.float32)
            if first:
                acc[rows, :] = part
            else:
                acc[rows, :] += part
            return carry

        lax.fori_loop(0, TOKENS // 256, tile, 0)

    w_go(9, rep, "B", east_dev)
    w_go(10, rep, "B", west_dev)
    w_go(0, rep, "A", y_dev)
    w_go(1, rep, "A", east_dev)
    w_go(2, rep, "A", west_dev)
    w_go(11, rep, "B", y_dev)
    project(rep, True)
    w_got(9, mine + west, "B")
    w_go(12, mine + west, "B0", east_dev)
    w_go(14, mine + west, "B", y_dev)
    w_got(10, mine + east, "B")
    w_go(13, mine + east, "B1", west_dev)
    w_go(15, mine + east, "B", y_dev)
    w_got(0, rep_y, "A")
    w_go(3, rep_y, "A", east_dev)
    w_go(4, rep_y, "A", west_dev)
    w_got(1, mine + west, "A")
    w_go(5, mine + west, "A0", east_dev)
    w_got(2, mine + east, "A")
    w_go(6, mine + east, "A1", west_dev)
    project(mine + west)
    project(mine + east)
    w_got(12, mine + far, "B0")
    w_go(16, mine + far, "B0", y_dev)
    w_got(13, mine + far, "B1")
    w_go(17, mine + far, "B1", y_dev)
    w_got(11, rep_y, "B")
    project(rep_y)
    w_got(3, across + west, "A")
    w_go(7, across + west, "A0", east_dev)
    w_got(4, across + east, "A")
    w_go(8, across + east, "A1", west_dev)

    o_go(11, rep, "B", y_dev, o_b)
    o_got(9, mine + west, "B")
    o_got(10, mine + east, "B")
    o_got(0, rep_y, "A")
    o_got(1, mine + west, "A")
    o_got(2, mine + east, "A")
    o_go(12, mine + west, "B0", east_dev)
    o_go(13, mine + east, "B1", west_dev)
    o_go(14, mine + west, "B", y_dev)
    o_go(15, mine + east, "B", y_dev)
    o_go(3, rep_y, "A", east_dev)
    o_go(4, rep_y, "A", west_dev)
    o_go(5, mine + west, "A0", east_dev)
    o_go(6, mine + east, "A1", west_dev)

    w_got(14, across + west, "B")
    project(across + west)
    w_got(15, across + east, "B")
    project(across + east)
    w_got(5, mine + far, "A0")
    w_got(6, mine + far, "A1")
    project(mine + far)
    w_got(7, across + far, "A0")
    w_got(8, across + far, "A1")
    w_got(16, across + far, "B0")
    w_got(17, across + far, "B1")
    project(across + far)

    def rotate(block, rows):
        return block * cosine[rows, :] + pltpu.roll(block, HD // 2, 1) * sine[rows, :]

    is_key = tp % 2 == 0
    for step in range(STEPS):
        rows = pl.ds(step * ROWS, ROWS)
        block = acc[rows, QC:WC]
        pair[0, rows, :] = jnp.where(is_key, rotate(block, rows), block).astype(jnp.bfloat16)
    send(pair.at[0], pair.at[1], pair_send, pair_recv, 0, (rep, core_peer))
    for step in range(STEPS):
        rows = pl.ds(step * ROWS, ROWS)
        for h in range(QC // HD):
            queries[:, step * 4 + h, :] = rotate(acc[rows, h * HD : (h + 1) * HD], rows)
    receive(pair.at[1], pair_send, pair_recv, 0)
    key_load.wait()
    value_load.wait()
    zeros = jnp.zeros((ROWS, 16, HD), jnp.float32)
    for place, target in ((0, keys), (1, values)):
        spread[...] = zeros
        slot = (tp + place) % 2
        for step in range(STEPS):
            spread[:, step, :] = pair[slot, pl.ds(step * ROWS, ROWS), :].astype(jnp.float32)
        target[:, pl.ds(CACHE, 16), :] = spread[...].astype(jnp.bfloat16)

    column = lax.broadcasted_iota(jnp.int32, (16, KEYS), 1)
    step_of = lax.broadcasted_iota(jnp.int32, (16, KEYS), 0) // 4
    new_ok = (column >= CACHE) & (column - CACHE <= step_of)
    score_scale = 1.0 / (float(HD) ** 0.5)

    def attend(chunk):
        def rows_of_8(it, carry):
            for u in range(8):
                local = it * 8 + u
                i = chunk * CROWS + local
                query = queries[i].astype(jnp.bfloat16)
                scores = lax.dot_general(
                    query, keys[i], (((1,), (1,)), ((), ())), preferred_element_type=jnp.float32
                )
                valid = (column < jnp.minimum(lens[i], CACHE)) | new_ok
                scores = jnp.where(valid, scores * score_scale, -1e30)
                top = jnp.max(scores, axis=-1, keepdims=True)
                weight = jnp.exp(scores - top)
                total = jnp.sum(weight, axis=-1, keepdims=True)
                probs = (weight / total).astype(jnp.bfloat16)
                attn_rows[local] = jnp.dot(probs, values[i], preferred_element_type=jnp.float32)
            return carry

        lax.fori_loop(0, CROWS // 8, rows_of_8, 0)
        for step in range(STEPS):
            for h in range(QC // HD):
                gathered[
                    tp,
                    pl.ds(chunk * CTOK + step * CROWS, CROWS),
                    pl.ds(h * HD, HD),
                ] = attn_rows[:, step * 4 + h, :].astype(jnp.bfloat16)

    def attn_block(t, chunk, part="all"):
        start, size = {"all": (0, CTOK), "0": (0, CTOK // 2), "1": (CTOK // 2, CTOK // 2)}[part]
        return gathered.at[t, pl.ds(chunk * CTOK + start, size), :]

    z_up, z_down, z_far = (z + 1) % 4 * 4, (z + 3) % 4 * 4, (z + 2) % 4 * 4
    low_hi = hi_peer % 4
    up_dev, down_dev = (rep, z_up + low), (rep, z_down + low)
    hi_dev, core_dev = (rep, hi_peer), (rep, core_peer)
    PER = 18

    def a_go(chunk, k, t, to, part="all"):
        block = attn_block(t, chunk, part)
        send(block, block, attn_send, attn_recv, chunk * PER + k, to)

    def a_got(chunk, k, t, part="all"):
        receive(attn_block(t, chunk, part), attn_send, attn_recv, chunk * PER + k)

    def gather_first(chunk):
        a_go(chunk, 0, tp, hi_dev)
        a_go(chunk, 1, tp, up_dev)
        a_go(chunk, 2, tp, down_dev)
        a_go(chunk, 3, tp, core_dev)

    def gather_second(chunk):
        a_got(chunk, 0, hi_peer)
        a_go(chunk, 4, hi_peer, up_dev)
        a_go(chunk, 5, hi_peer, down_dev)
        a_got(chunk, 1, z_down + low)
        a_go(chunk, 7, z_down + low, up_dev, "0")
        a_got(chunk, 2, z_up + low)
        a_go(chunk, 8, z_up + low, down_dev, "1")
        a_go(chunk, 6, hi_peer, core_dev)
        a_go(chunk, 9, z_down + low, core_dev)
        a_go(chunk, 10, z_up + low, core_dev)

    def gather_third(chunk):
        a_got(chunk, 4, z_down + low_hi)
        a_go(chunk, 11, z_down + low_hi, up_dev, "0")
        a_got(chunk, 5, z_up + low_hi)
        a_go(chunk, 12, z_up + low_hi, down_dev, "1")
        a_go(chunk, 13, z_down + low_hi, core_dev)
        a_go(chunk, 14, z_up + low_hi, core_dev)
        a_got(chunk, 7, z_far + low, "0")
        a_got(chunk, 8, z_far + low, "1")
        a_go(chunk, 15, z_far + low, core_dev)

    def gather_fourth(chunk):
        a_got(chunk, 11, z_far + low_hi, "0")
        a_got(chunk, 12, z_far + low_hi, "1")
        a_go(chunk, 16, z_far + low_hi, core_dev)

    low_core = core_peer % 4
    low_both = (low_hi + 1) - 2 * (low_hi % 2)

    def gather_last(chunk):
        a_got(chunk, 3, core_peer)
        a_got(chunk, 6, z * 4 + low_both)
        a_got(chunk, 9, z_down + low_core)
        a_got(chunk, 10, z_up + low_core)
        a_got(chunk, 13, z_down + low_both)
        a_got(chunk, 14, z_up + low_both)
        a_got(chunk, 15, z_far + low_core)
        a_got(chunk, 16, z_far + low_both)

    attend(0)
    gather_first(0)
    o_got(12, mine + far, "B0")
    o_go(16, mine + far, "B0", y_dev)
    o_got(13, mine + far, "B1")
    o_go(17, mine + far, "B1", y_dev)
    attend(1)
    gather_first(1)
    gather_second(0)
    attend(2)
    gather_first(2)
    gather_second(1)
    gather_third(0)
    o_got(3, across + west, "A")
    o_go(7, across + west, "A0", east_dev)
    o_got(4, across + east, "A")
    o_go(8, across + east, "A1", west_dev)
    attend(3)
    gather_first(3)
    gather_second(2)
    gather_third(1)
    gather_fourth(0)
    gather_second(3)
    gather_third(2)
    gather_fourth(1)
    gather_third(3)
    gather_fourth(2)
    gather_fourth(3)

    out_load.wait()
    o_got(5, mine + far, "A0")
    o_got(6, mine + far, "A1")
    o_got(11, rep_y, "B")
    o_got(14, across + west, "B")
    o_got(15, across + east, "B")
    o_got(7, across + far, "A0")
    o_got(8, across + far, "A1")
    o_got(16, across + far, "B0")
    o_got(17, across + far, "B1")
    for chunk in range(CHUNKS):
        gather_last(chunk)

    out_acc[...] = jnp.zeros_like(out_acc)

    def out_step(t, carry):
        cols = pl.ds(pl.multiple_of(t * QC, QC), QC)
        out_acc[...] += lax.dot_general(
            gathered[t], out_rows[:, cols], (((1,), (1,)), ((), ())), preferred_element_type=jnp.float32
        )
        return carry

    lax.fori_loop(0, TP, out_step, 0)

    residual_load.wait()
    for chunk in range(CHUNKS):
        rows = pl.ds(chunk * CROWS, CROWS)
        ends = finish[rows, :]
        picked = jnp.zeros((CROWS, QC), jnp.float32)
        for step in range(STEPS):
            total = out_acc[pl.ds(chunk * CTOK + step * CROWS, CROWS), :]
            total = total + residual[step, rows, :].astype(jnp.float32)
            kept = jnp.where(ends >= step, total, 0.0).astype(jnp.bfloat16)
            decoded[step, rows, :] = kept
            picked = jnp.where(ends == step, kept.astype(jnp.float32), picked)
        at_finish[rows, :] = picked.astype(jnp.bfloat16)

    outgoing[...] = jnp.dot(
        one_hot[...], at_finish[...], preferred_element_type=jnp.float32
    ).astype(jnp.bfloat16)
    for d in range(1, TP):
        to = (tp + d) % TP
        send(
            outgoing.at[pl.ds(pl.multiple_of(to * 16, 16), 16), :],
            stage_one.at[tp],
            one_send,
            one_recv,
            d,
            (rep, to),
        )
    stage_one[tp] = outgoing[pl.ds(pl.multiple_of(tp * 16, 16), 16), :]
    for d in range(1, TP):
        receive(stage_one.at[(tp + TP - d) % TP], one_send, one_recv, d)
    for t in range(TP):
        for part in range(QC // HD):
            arrived[:, t * 4 + part, :] = stage_one[t, :, part * HD : (part + 1) * HD].astype(jnp.float32)
    stage_two[0] = arrived[...].astype(jnp.bfloat16)
    for d in range(1, REP):
        to = (rep + d) % REP
        send(
            stage_two.at[0, pl.ds(to * 2, 2)],
            stage_two.at[1, pl.ds(rep * 2, 2)],
            two_send,
            two_recv,
            d,
            (to, tp),
        )
    stage_two[1, pl.ds(rep * 2, 2)] = stage_two[0, pl.ds(rep * 2, 2)]
    for d in range(1, REP):
        receive(stage_two.at[1, pl.ds((rep + REP - d) % REP * 2, 2)], two_send, two_recv, d)
    for rank in range(2):
        for r in range(REP):
            arrived[rank * REP + r] = stage_two[1, r * 2 + rank].astype(jnp.float32)
    for part in range(D // HD):
        returned[:, part * HD : (part + 1) * HD] = arrived[:, part, :].astype(jnp.bfloat16)

    for copy in pending:
        copy.wait_send()


def per_device(
    hidden,
    norm_gain,
    q_weight,
    k_weight,
    v_weight,
    o_weight,
    key_cache,
    value_cache,
    cache_len,
    finish,
    owner,
):
    positions = cache_len[None, :] + jnp.arange(STEPS, dtype=jnp.int32)[:, None]
    half = HD // 2
    freqs = 500000.0 ** (-(jnp.arange(half, dtype=jnp.float32) * 2.0) / HD)
    angles = (positions.astype(jnp.float32)[..., None] * freqs).reshape(TOKENS, half)
    cosine, sine = jnp.cos(angles), jnp.sin(angles)
    cosine = jnp.concatenate([cosine, cosine], axis=-1)
    sine = jnp.concatenate([-sine, sine], axis=-1)

    owner_flat = owner[:, 0]
    is_returned = finish < STEPS
    row_ids = jnp.arange(ROWS)
    same = (
        (owner_flat[:, None] == owner_flat[None, :])
        & is_returned[None, :]
        & (row_ids[None, :] < row_ids[:, None])
    )
    rank = jnp.sum(same.astype(jnp.int32), axis=1)
    slot = (owner_flat % TP) * (REP * 2) + (owner_flat // TP) * 2 + rank
    slot = jnp.where(is_returned, slot, -1)
    one_hot = (jnp.arange(REP * TP * 2)[:, None] == slot[None, :]).astype(jnp.bfloat16)

    hbm = pl.BlockSpec(memory_space=pl.ANY)
    vmem = pl.BlockSpec(memory_space=pltpu.VMEM)
    smem = pl.BlockSpec(memory_space=pltpu.SMEM)
    dma = pltpu.SemaphoreType.DMA
    bf16, f32 = jnp.bfloat16, jnp.float32
    return pl.pallas_call(
        kernel,
        out_shape=(
            jax.ShapeDtypeStruct((STEPS, ROWS, QC), bf16),
            jax.ShapeDtypeStruct((16, D), bf16),
        ),
        in_specs=[hbm, vmem, hbm, hbm, hbm, hbm, hbm, hbm, smem, vmem, vmem, vmem, vmem],
        out_specs=(vmem, vmem),
        scratch_shapes=[
            pltpu.VMEM((2, CROWS, D), bf16),
            pltpu.VMEM((REP, TOKENS, BLOCK), bf16),
            pltpu.VMEM((REP, BLOCK, WC), bf16),
            pltpu.VMEM((REP * SHARD, D), bf16),
            pltpu.VMEM((ROWS, KEYS, HD), bf16),
            pltpu.VMEM((ROWS, KEYS, HD), bf16),
            pltpu.VMEM((TOKENS, WC), f32),
            pltpu.VMEM((ROWS, 16, HD), f32),
            pltpu.VMEM((2, TOKENS, HD), bf16),
            pltpu.VMEM((CROWS, 16, HD), f32),
            pltpu.VMEM((TP, TOKENS, QC), bf16),
            pltpu.VMEM((TOKENS, QC), f32),
            pltpu.VMEM((STEPS, ROWS, QC), bf16),
            pltpu.VMEM((ROWS, QC), bf16),
            pltpu.VMEM((256, QC), bf16),
            pltpu.VMEM((TP, 16, QC), bf16),
            pltpu.VMEM((ROWS, 16, HD), f32),
            pltpu.VMEM((2, 16, D // HD, HD), bf16),
            pltpu.VMEM((16, D // HD, HD), f32),
            dma((2,)),
            dma((6,)),
            dma((2 * TP,)),
            dma((2 * TP,)),
            dma((18,)),
            dma((18,)),
            dma((18,)),
            dma((18,)),
            dma((1,)),
            dma((1,)),
            dma((18 * CHUNKS,)),
            dma((18 * CHUNKS,)),
            dma((TP,)),
            dma((TP,)),
            dma((REP,)),
            dma((REP,)),
        ],
        compiler_params=pltpu.CompilerParams(
            collective_id=0, has_side_effects=True, vmem_limit_bytes=60 * 1024 * 1024
        ),
    )(
        hidden,
        norm_gain.reshape(1, D),
        q_weight,
        k_weight,
        v_weight,
        o_weight,
        key_cache,
        value_cache,
        cache_len,
        finish.reshape(ROWS, 1),
        cosine,
        sine,
        one_hot,
    )


def solution(mesh):
    placed = (
        P(None, "rep", None),
        P(),
        P(("rep", "tp"), None),
        P(("rep", "tp"), None),
        P(("rep", "tp"), None),
        P(("tp", "rep"), None),
        P("rep", "tp", None, None),
        P("rep", "tp", None, None),
        P("rep"),
        P("rep"),
        P("rep", None),
    )
    return jax.shard_map(
        per_device,
        mesh=mesh,
        in_specs=placed,
        out_specs=(P(None, "rep", "tp"), P(("rep", "tp"), None)),
        check_vma=False,
    )
```

time: 390 us -> 215 us (0.55)
  Pallas kernels: 0 us -> 201 us
  waiting for transfers between devices: 191 us -> 0 us
  blocking collectives: 97.5 us -> 0 us
  matrix products: 35.4 us -> 0 us
  other arithmetic: 31.5 us -> 4.91 us
  between operations: 14.1 us -> 0.66 us
  local copies, waits for them, and re-layouts: 19.3 us -> 6.93 us
    pallas_call x0 -> x1, Pallas kernels: none -> 201 us  [per_device(): pl.pallas_call(kernel, out_shape=(jax.ShapeDtypeStruct((STEPS, ROWS, QC),...]
    all_gather x4 -> x0, waiting for transfers between devices: 190 us -> none  [the longest x1 79.3 us: per_device(): attended_full = lax.all_gather(attended, 'tp', axis=1, tiled=True)]
    all_to_all x3 -> x0, blocking collectives: 97.5 us -> none  [the longest x1 60.6 us: per_device(): lax.all_to_all(q_weight, 'tp', split_axis=1, concat_axis=0, tiled=True)]
    dot_general x8 -> x0, matrix products: 35.4 us -> none  [the longest x1 9.51 us: per_device(): lax.dot_general(attended_full, out_rows, (((1,), (1,)), ((), ())), prefer...]
    convert_element_type x3 -> x1, other arithmetic: 21.3 us -> 0.65 us  [per_device(): (jnp.arange(REP * TP * 2)[:, None] == slot[None, :]).astype(jnp.bfloat16)]
    dot_general x1 -> x0, local copies, waits for them, and re-layouts: 11.8 us -> none  [per_device(): jnp.dot(normed_flat, query_full, preferred_element_type=jnp.float32)]
    reduce_sum x4 -> x0, other arithmetic: 8.76 us -> none  [the longest x1 5.1 us: per_device(): mean_square = jnp.mean(hidden_f * hidden_f, axis=-1, keepdims=True)]
  transfers between devices with their start and end apart: 4 -> 0, of which waited for: 3 -> 0; matrix products, arithmetic and copies ran while one was open for 18% -> 0% of each run, Pallas kernels for 0% -> 0%
where the time goes in v2:
time: 215 us; the launch traced here: 214 us
  Pallas kernels  201 us (93%)
  local copies, waits for them, and re-layouts  6.93 us (3%)
  other arithmetic  4.91 us (2%)
    pallas_call x1, Pallas kernels, per_device(): pl.pallas_call(kernel, out_shape=(jax.ShapeDtypeStruct((STEPS, ROWS, QC),...  201 us

profile of v2, /device:TPU:1, one launch (start us, length us, event | category | flops | bytes accessed | tf_op | source)
XLA Modules:
  0.0 213.6 jit_solution(8349310438004306939)
XLA Ops:
  0.6 0.7 broadcast_compare_fusion
  1.3 0.9 convert_reduce_fusion
  2.2 0.7 fusion.7
  2.9 0.7 add.34
  3.6 1.3 reshape.41.gain
  4.9 0.6 fusion.one_hot
  5.6 1.4 copy.14.finish
  7.0 1.0 fusion.1
  8.0 1.0 pad_maximum_fusion
  9.0 201.1 %shard_map.122 = (bf16[4,128,512]{2,1,0:T(8,128)(2,1)}, bf16[16,8192]{1,0:T(8,128)(2,1)}) custom-call(bf16[4,128,8192]{2,1,0:T(8,128)(2,1)} %hidden.1, bf16[1,8192]{1,0:T(2,128)(2,1)} %reshape.41.gain, bf16[64,8192]{1,0:T(8,128)(2,1)} %q_weight.1, bf16[64,1024]{1,0:T(8,128)(2,1)} %k_weight.1, bf16[64,1024]{1,0:T(8,128)(2,1)} %v_weight.1, ...), custom_call_target="tpu_custom_call" | custom-call | tf_op jit(solution)/shard_map/pallas_call | solution.py:609
  210.1 1.9 copy.17
  212.0 1.7 copy.18
  (2 shorter events, 0.0 us)

commit v3 on v2

v3 whole, which is shorter than its diff:
```python
import jax
import jax.numpy as jnp
import numpy as np
from jax import lax
from jax.experimental import pallas as pl
from jax.experimental.pallas import tpu as pltpu
from jax.sharding import PartitionSpec as P

MESH = pl.DeviceIdType.MESH
KV = 8
STEPS = 4
ROWS = 128
HD = 128
CACHE = 192
KEYS = CACHE + 16
D = 8192
REP = 8
TP = 16
QC = 512
WC = QC + HD
SHARD = 64
BLOCK = TP * SHARD
TOKENS = STEPS * ROWS
CHUNKS = 4
SLOTS = 4
CROWS = ROWS // CHUNKS
HALF_ROWS = ROWS // 2
HALF_TOKENS = HALF_ROWS * STEPS
EPS = 1e-05

STAGES = ((0, 384), (384, 256))
OUT_CUT = 5120


def kernel(
    hidden,
    gain,
    q_weight,
    k_weight,
    v_weight,
    o_weight,
    key_cache,
    value_cache,
    lens,
    lens_row,
    finish_row,
    owner,
    frequency,
    decoded,
    returned,
    staged,
    shared,
    normed,
    weights,
    out_rows,
    keys,
    values,
    acc,
    queries,
    partial,
    pair,
    attn_rows,
    gathered,
    out_acc,
    residual,
    cosine,
    sine,
    one_hot,
    ends,
    limits,
    at_finish,
    outgoing,
    stage_one,
    spread,
    stage_two,
    arrived,
    load_sem,
    local_sem,
    a2a_send,
    a2a_recv,
    norm_send,
    norm_recv,
    qkv_send,
    qkv_recv,
    part_send,
    part_recv,
    out_send,
    out_recv,
    pair_send,
    pair_recv,
    attn_send,
    attn_recv,
    one_send,
    one_recv,
    two_send,
    two_recv,
):
    rep = lax.axis_index("rep")
    tp = lax.axis_index("tp")
    y, x = rep // 4, rep % 4
    across = (1 - y) * 4
    mine = y * 4
    east, west, far = (x + 1) % 4, (x + 3) % 4, (x + 2) % 4
    rep_east, rep_west, rep_y = mine + east, mine + west, across + x
    z, low = tp // 4, tp % 4
    core_peer = tp + 1 - 2 * (tp % 2)
    hi_peer = tp + 2 - 4 * ((tp // 2) % 2)
    pending = []

    def send(src, dst, sends, recvs, k, to):
        copy = pltpu.make_async_remote_copy(
            src_ref=src,
            dst_ref=dst,
            send_sem=sends.at[k],
            recv_sem=recvs.at[k],
            device_id=to,
            device_id_type=MESH,
        )
        copy.start()
        pending.append(copy)

    def receive(region, sends, recvs, k):
        pltpu.make_async_remote_copy(
            src_ref=region,
            dst_ref=region,
            send_sem=sends.at[k],
            recv_sem=recvs.at[k],
            device_id=(rep, core_peer),
            device_id_type=MESH,
        ).wait_recv()

    barrier = pltpu.get_barrier_semaphore()
    for d in range(1, TP):
        pl.semaphore_signal(
            barrier, inc=1, device_id=(rep, (tp + d) % TP), device_id_type=MESH
        )
    for d in range(1, REP):
        pl.semaphore_signal(
            barrier, inc=1, device_id=((rep + d) % REP, tp), device_id_type=MESH
        )
    key_load = pltpu.make_async_copy(
        key_cache.at[:, 0], keys.at[:, pl.ds(0, CACHE), :], local_sem.at[0]
    )
    value_load = pltpu.make_async_copy(
        value_cache.at[:, 0], values.at[:, pl.ds(0, CACHE), :], local_sem.at[1]
    )
    my_cols = pl.ds(pl.multiple_of(tp * QC, QC), QC)
    residual_load = pltpu.make_async_copy(
        hidden.at[:, :, my_cols], residual, local_sem.at[2]
    )
    my_rows = pl.ds(pl.multiple_of(tp * SHARD, SHARD), SHARD)
    q_load = pltpu.make_async_copy(
        q_weight.at[:, my_cols], weights.at[x, my_rows, pl.ds(HD, QC)], local_sem.at[3]
    )
    kv_cols = pl.ds(pl.multiple_of((tp // 2) * HD, HD), HD)
    my_kv = weights.at[x, my_rows, pl.ds(0, HD)]
    k_load = pltpu.make_async_copy(k_weight.at[:, kv_cols], my_kv, local_sem.at[4])
    v_load = pltpu.make_async_copy(v_weight.at[:, kv_cols], my_kv, local_sem.at[4])

    def out_block(r, part):
        start, size = {
            "A": (0, OUT_CUT),
            "A0": (0, OUT_CUT // 2),
            "A1": (OUT_CUT // 2, OUT_CUT // 2),
            "B": (OUT_CUT, D - OUT_CUT),
            "B0": (OUT_CUT, (D - OUT_CUT) // 2),
            "B1": (OUT_CUT + (D - OUT_CUT) // 2, (D - OUT_CUT) // 2),
            "all": (0, D),
        }[part]
        return out_rows.at[
            pl.ds(pl.multiple_of(r * SHARD, SHARD), SHARD), pl.ds(start, size)
        ]

    out_load = pltpu.make_async_copy(o_weight, out_block(rep, "all"), local_sem.at[5])
    q_load.start()
    pl.when(tp % 2 == 0)(k_load.start)
    pl.when(tp % 2 == 1)(v_load.start)
    out_load.start()

    def hidden_load(step, slot):
        return pltpu.make_async_copy(
            hidden.at[step // CHUNKS, pl.ds(pl.multiple_of((step % CHUNKS) * CROWS, CROWS), CROWS), :],
            staged.at[slot],
            load_sem.at[slot],
        )

    hidden_load(tp, SLOTS).start()
    for step in range(SLOTS - 1):
        hidden_load(step, step).start()
    def norm_rows(slot, half, part, store):
        part_rows = pl.ds(pl.multiple_of(part * 16, 16), 16)
        values_f = staged[slot, part_rows, :].astype(jnp.float32)
        mean = jnp.mean(values_f * values_f, axis=-1, keepdims=True)
        scale = lax.rsqrt(mean + EPS)
        for b in range(4):
            cols = pl.ds(pl.multiple_of(half * (D // 2) + b * BLOCK, BLOCK), BLOCK)
            block = staged[slot, part_rows, cols].astype(jnp.float32)
            block = block * scale * gain[:, cols].astype(jnp.float32)
            store(b, block.astype(jnp.bfloat16))

    def norm_step(step, carry):
        slot = step % SLOTS
        hidden_load(step, slot).wait()

        @pl.when(step + SLOTS - 1 < STEPS * CHUNKS)
        def _():
            hidden_load(step + SLOTS - 1, (step + SLOTS - 1) % SLOTS).start()

        def sixteen(part, carry):
            rows = pl.ds(pl.multiple_of(step * CROWS + part * 16, 16), 16)

            def store(b, block):
                normed[0, b, rows, :] = block

            norm_rows(slot, y, part, store)
            return carry

        return lax.fori_loop(0, CROWS // 16, sixteen, carry)

    with jax.named_scope("norm_shared"):
        hidden_load(tp, SLOTS).wait()

        def sixteen_shared(part, carry):
            rows = pl.ds(pl.multiple_of(part * 16, 16), 16)

            def store(b, block):
                shared[b, rows, :] = block

            norm_rows(SLOTS, 1 - y, part, store)
            return carry

        lax.fori_loop(0, CROWS // 16, sixteen_shared, 0)

    def norm_block(t, part):
        start, size = {"all": (0, 4), "0": (0, 2), "1": (2, 2)}[part]
        rows = pl.ds(pl.multiple_of(t * CROWS, CROWS), CROWS)
        return normed.at[1, pl.ds(start, size), rows, :]

    with jax.named_scope("greet"):
        pl.semaphore_wait(barrier, TP - 1 + REP - 1)

    q_parts = ((0, STAGES[0][1] - HD), (STAGES[0][1] - HD, STAGES[1][1]))
    def a2a_go(stage):
        start, size = q_parts[stage]
        for d in range(1, TP):
            to = (tp + d) % TP
            there = (rep, to)
            send(
                q_weight.at[:, pl.ds(pl.multiple_of(to * QC + start, HD), size)],
                weights.at[x, my_rows, pl.ds(HD + start, size)],
                a2a_send,
                a2a_recv,
                (1 + stage) * TP + d,
                there,
            )
            if stage == 1:
                continue
            cols = pl.ds(pl.multiple_of((to // 2) * HD, HD), HD)

            def kv_copy(source, cols=cols, d=d, there=there):
                return pltpu.make_async_remote_copy(
                    src_ref=source.at[:, cols],
                    dst_ref=weights.at[x, my_rows, pl.ds(0, HD)],
                    send_sem=a2a_send.at[d],
                    recv_sem=a2a_recv.at[d],
                    device_id=there,
                    device_id_type=MESH,
                )

            from_k, from_v = kv_copy(k_weight), kv_copy(v_weight)
            pl.when(to % 2 == 0)(from_k.start)
            pl.when(to % 2 == 1)(from_v.start)
            pending.append(from_k)

    def a2a_got(stage):
        start, size = q_parts[stage]
        for d in range(1, TP):
            source = (tp + TP - d) % TP
            rows = pl.ds(pl.multiple_of(source * SHARD, SHARD), SHARD)
            receive(weights.at[x, rows, pl.ds(HD + start, size)], a2a_send, a2a_recv, (1 + stage) * TP + d)
            if stage == 0:
                receive(weights.at[x, rows, pl.ds(0, HD)], a2a_send, a2a_recv, d)

    east_dev, west_dev, y_dev = (rep_east, tp), (rep_west, tp), (rep_y, tp)

    def o_go(k, r, part, to, src=None):
        dst = out_block(r, part)
        send(dst if src is None else src, dst, out_send, out_recv, k, to)

    def o_got(k, r, part):
        receive(out_block(r, part), out_send, out_recv, k)

    o_a = o_weight.at[:, pl.ds(0, OUT_CUT)]
    o_b = o_weight.at[:, pl.ds(OUT_CUT, D - OUT_CUT)]

    z_up, z_down, z_far = (z + 1) % 4 * 4, (z + 3) % 4 * 4, (z + 2) % 4 * 4
    low_hi, low_core = hi_peer % 4, core_peer % 4
    low_both = low_hi + 1 - 2 * (low_hi % 2)
    up_dev, down_dev = (rep, z_up + low), (rep, z_down + low)
    hi_dev, core_dev = (rep, hi_peer), (rep, core_peer)

    class TpGather:
        def __init__(self, block, sends, recvs, base):
            self.block, self.sends, self.recvs, self.base = block, sends, recvs, base

        def go(self, k, t, to, part="all"):
            block = self.block(t, part)
            send(block, block, self.sends, self.recvs, self.base + k, to)

        def got(self, k, t, part="all"):
            receive(self.block(t, part), self.sends, self.recvs, self.base + k)

        def first(self):
            self.go(0, tp, hi_dev)
            self.go(1, tp, up_dev)
            self.go(2, tp, down_dev)
            self.go(3, tp, core_dev)

        def second(self):
            self.got(0, hi_peer)
            self.go(4, hi_peer, up_dev)
            self.go(5, hi_peer, down_dev)
            self.got(1, z_down + low)
            self.go(7, z_down + low, up_dev, "0")
            self.got(2, z_up + low)
            self.go(8, z_up + low, down_dev, "1")
            self.go(6, hi_peer, core_dev)
            self.go(9, z_down + low, core_dev)
            self.go(10, z_up + low, core_dev)

        def third(self):
            self.got(4, z_down + low_hi)
            self.go(11, z_down + low_hi, up_dev, "0")
            self.got(5, z_up + low_hi)
            self.go(12, z_up + low_hi, down_dev, "1")
            self.go(13, z_down + low_hi, core_dev)
            self.go(14, z_up + low_hi, core_dev)
            self.got(7, z_far + low, "0")
            self.got(8, z_far + low, "1")
            self.go(15, z_far + low, core_dev)

        def fourth(self):
            self.got(11, z_far + low_hi, "0")
            self.got(12, z_far + low_hi, "1")
            self.go(16, z_far + low_hi, core_dev)

        def near(self):
            self.got(3, core_peer)
            self.got(6, z * 4 + low_both)
            self.got(9, z_down + low_core)
            self.got(10, z_up + low_core)
            self.got(13, z_down + low_both)
            self.got(14, z_up + low_both)

        def rest(self):
            self.got(15, z_far + low_core)
            self.got(16, z_far + low_both)

    norm_gather = TpGather(norm_block, norm_send, norm_recv, 0)
    send(shared, norm_block(tp, "all"), norm_send, norm_recv, 17, y_dev)
    a2a_go(0)
    a2a_go(1)
    o_go(9, rep, "B", east_dev, o_b)
    o_go(10, rep, "B", west_dev, o_b)

    with jax.named_scope("tables"):
        square = (ROWS, ROWS)
        rows_at = lax.broadcasted_iota(jnp.int32, square, 0)
        cols_at = lax.broadcasted_iota(jnp.int32, square, 1)

        def flip(values):
            return values.astype(jnp.float32).T.astype(jnp.int32)

        lens_col = jnp.broadcast_to(lens_row[...].astype(jnp.float32).reshape(1, ROWS), square).T
        finish_cols = jnp.broadcast_to(finish_row[...].reshape(1, ROWS), square)
        finish_rows = flip(finish_cols)
        ends[...] = finish_rows
        owner_rows = jnp.broadcast_to(owner[...], square)
        owner_cols = flip(owner_rows)
        sign = jnp.where(cols_at < HD // 2, -1.0, 1.0)
        for step in range(STEPS):
            angles = (lens_col + float(step)) * frequency[...]
            cosine[pl.ds(step * ROWS, ROWS), :] = jnp.cos(angles)
            sine[pl.ds(step * ROWS, ROWS), :] = jnp.sin(angles) * sign
        same = (owner_rows == owner_cols) & (finish_rows < STEPS) & (rows_at < cols_at)
        rank = jnp.sum(jnp.where(same, 1.0, 0.0), axis=0, keepdims=True).astype(jnp.int32)
        owner_row = owner_cols[0:1, :]
        slot = (owner_row % TP) * (REP * 2) + (owner_row // TP) * 2 + rank
        slot = jnp.where(finish_cols[0:1, :] < STEPS, slot, -1)
        slots_at = lax.broadcasted_iota(jnp.int32, (REP * TP * 2, ROWS), 0)
        one_hot[...] = jnp.where(slots_at == slot, 1.0, 0.0).astype(jnp.bfloat16)
        key_at = lax.broadcasted_iota(jnp.int32, (KEYS, HD), 0)
        step_at = lax.broadcasted_iota(jnp.int32, (KEYS, HD), 1) % 8 // 2
        new_at = jnp.where(key_at - CACHE <= step_at, -1, 4 * CACHE)
        limits[...] = jnp.where(key_at < CACHE, key_at, new_at)

    def ring_block(stage, b, half):
        start, size = STAGES[stage]
        return weights.at[b, pl.ds(half * (BLOCK // 2), BLOCK // 2), pl.ds(start, size)]

    def w_go(stage, k, b, half, to):
        block = ring_block(stage, b, half)
        send(block, block, qkv_send, qkv_recv, stage * 6 + k, to)

    def w_got(stage, k, b, half):
        receive(ring_block(stage, b, half), qkv_send, qkv_recv, stage * 6 + k)

    def ring_own(stage):
        w_go(stage, 0, x, 0, east_dev)
        w_go(stage, 1, x, 1, west_dev)
        w_go(stage, 2, x, 1, east_dev)
        w_go(stage, 3, x, 0, west_dev)

    def ring_on(stage):
        w_got(stage, 0, west, 0)
        w_go(stage, 4, west, 0, east_dev)
        w_got(stage, 1, east, 1)
        w_go(stage, 5, east, 1, west_dev)

    def ring_near(stage):
        w_got(stage, 2, west, 1)
        w_got(stage, 3, east, 0)

    def ring_far(stage):
        w_got(stage, 4, far, 0)
        w_got(stage, 5, far, 1)

    def project(stage, which, b, first=False):
        start, size = STAGES[stage]

        def tile(m, carry):
            rows = pl.ds(pl.multiple_of(m * 256, 256), 256)
            part = jnp.dot(
                normed[which, b, rows, :],
                weights[b, :, start : start + size],
                preferred_element_type=jnp.float32,
            )
            if first:
                acc[which, rows, start : start + size] = part
            else:
                acc[which, rows, start : start + size] += part
            return carry

        lax.fori_loop(0, TOKENS // 256, tile, 0)

    def part_block(which, stage):
        start, size = STAGES[stage]
        return partial.at[which, :, pl.ds(start, size)]

    def part_go(stage):
        start, size = STAGES[stage]
        partial[0, :, start : start + size] = acc[1, :, start : start + size].astype(jnp.bfloat16)
        send(part_block(0, stage), part_block(1, stage), part_send, part_recv, stage, y_dev)

    def part_got(stage):
        receive(part_block(1, stage), part_send, part_recv, stage)

    with jax.named_scope("norm_over_y"):
        receive(norm_block(tp, "all"), norm_send, norm_recv, 17)
        norm_gather.first()
    with jax.named_scope("a2a_wait"):
        q_load.wait()
        k_load.wait()
        a2a_got(0)
        ring_own(0)
        o_go(0, rep, "A", y_dev, o_a)
    with jax.named_scope("norm"):
        lax.fori_loop(0, 8, norm_step, 0)
    with jax.named_scope("norm_second"):
        norm_gather.second()
    with jax.named_scope("ring_on_0"):
        ring_on(0)
    with jax.named_scope("norm"):
        lax.fori_loop(8, 16, norm_step, 0)
    with jax.named_scope("ring_near_0"):
        ring_near(0)
        a2a_got(1)
        ring_own(1)
    with jax.named_scope("norm_third"):
        norm_gather.third()
    key_load.start()
    value_load.start()
    residual_load.start()
    with jax.named_scope("project"):
        project(0, 0, x, True)
        project(0, 0, west)
        project(0, 0, east)
    with jax.named_scope("norm_last"):
        norm_gather.fourth()
        norm_gather.near()
        norm_gather.rest()
    with jax.named_scope("project"):
        project(0, 1, x, True)
        project(0, 1, west)
        project(0, 1, east)
    with jax.named_scope("ring_far_0"):
        ring_far(0)
        project(0, 1, far)
        part_go(0)
        o_go(11, rep, "B", y_dev, o_b)
        o_got(9, mine + west, "B")
        o_got(10, mine + east, "B")
        project(0, 0, far)
    with jax.named_scope("ring_on_1"):
        ring_on(1)
    with jax.named_scope("project"):
        project(1, 0, x, True)
        project(1, 1, x, True)
    with jax.named_scope("out_first"):
        o_go(1, rep, "A", east_dev, o_a)
        o_go(2, rep, "A", west_dev, o_a)
        o_go(12, mine + west, "B0", east_dev)
        o_go(13, mine + east, "B1", west_dev)

    def rotate(block, rows):
        return block * cosine[rows, :] + pltpu.roll(block, HD // 2, 1) * sine[rows, :]

    def total(step, start):
        rows = pl.ds(step * ROWS, ROWS)
        cols = slice(start, start + HD)
        return acc[0, rows, cols] + partial[1, rows, cols].astype(jnp.float32)

    def place_queries(stage):
        for step in range(STEPS):
            rows = pl.ds(step * ROWS, ROWS)
            for h in range(2):
                start = HD + (stage * 2 + h) * HD
                queries[stage, :, step * 2 + h, :] = rotate(total(step, start), rows)

    is_key = tp % 2 == 0
    with jax.named_scope("keys"):
        part_got(0)
        for step in range(STEPS):
            rows = pl.ds(step * ROWS, ROWS)
            block = total(step, 0)
            pair[0, rows, :] = jnp.where(is_key, rotate(block, rows), block).astype(jnp.bfloat16)
        send(pair.at[0], pair.at[1], pair_send, pair_recv, 0, core_dev)
        place_queries(0)
    with jax.named_scope("ring_near_1"):
        ring_near(1)
    with jax.named_scope("project"):
        project(1, 1, west)
        project(1, 1, east)
        project(1, 0, west)
        project(1, 0, east)
    receive(pair.at[1], pair_send, pair_recv, 0)
    key_load.wait()
    value_load.wait()
    zeros = jnp.zeros((ROWS, 16, HD), jnp.float32)
    for place, target in ((0, keys), (1, values)):
        spread[...] = zeros
        slot = (tp + place) % 2
        for step in range(STEPS):
            spread[:, step, :] = pair[slot, pl.ds(step * ROWS, ROWS), :].astype(jnp.float32)
        target[:, pl.ds(CACHE, 16), :] = spread[...].astype(jnp.bfloat16)

    row_of = lax.broadcasted_iota(jnp.int32, (KEYS, HD), 1) // 8
    score_scale = 1.0 / (float(HD) ** 0.5)

    def attend(stage, half):
        def rows_of_16(it, carry):
            first = half * HALF_ROWS + it * 16
            query = queries[stage, pl.ds(first, 16)].reshape(16 * 8, HD).astype(jnp.bfloat16)
            scores = None
            valid = jnp.zeros((1, HD), jnp.int32)
            for u in range(16):
                part = lax.dot_general(
                    keys[first + u], query, (((1,), (1,)), ((), ())), preferred_element_type=jnp.float32
                )
                scores = part if scores is None else jnp.where(row_of == u, part, scores)
                valid = jnp.where(row_of[0:1, :] == u, lens[first + u], valid)
            scores = jnp.where(limits[...] < valid, scores, -1e30)
            top = jnp.max(scores, axis=0, keepdims=True)
            weight = jnp.exp((scores - top) * score_scale)
            total = jnp.sum(weight, axis=0, keepdims=True)
            probs = (weight * (1.0 / total)).T
            for u in range(16):
                attn_rows[it * 16 + u] = jnp.dot(
                    probs[u * 8 : (u + 1) * 8].astype(jnp.bfloat16),
                    values[first + u],
                    preferred_element_type=jnp.float32,
                )
            return carry

        lax.fori_loop(0, HALF_ROWS // 16, rows_of_16, 0)
        for step in range(STEPS):
            for h in range(2):
                gathered[
                    tp,
                    pl.ds(half * HALF_TOKENS + step * HALF_ROWS, HALF_ROWS),
                    pl.ds((stage * 2 + h) * HD, HD),
                ] = attn_rows[:, step * 2 + h, :].astype(jnp.bfloat16)

    def attn_block(t, chunk, part="all"):
        size = HALF_TOKENS // 2
        start, size = {"all": (0, HALF_TOKENS), "0": (0, size), "1": (size, size)}[part]
        rows = pl.ds(chunk % 2 * HALF_TOKENS + start, size)
        return gathered.at[t, rows, pl.ds(chunk // 2 * 2 * HD, 2 * HD)]

    PER = 18
    gathers = [
        TpGather(
            lambda t, part, chunk=chunk: attn_block(t, chunk, part), attn_send, attn_recv, chunk * PER
        )
        for chunk in range(CHUNKS)
    ]

    def attend_and_send(chunk):
        with jax.named_scope("attend"):
            attend(chunk // 2, chunk % 2)
        gathers[chunk].first()

    attend_and_send(0)
    with jax.named_scope("ring_far_1"):
        ring_far(1)
        project(1, 1, far)
        part_go(1)
        project(1, 0, far)
        o_go(14, mine + west, "B", y_dev)
    with jax.named_scope("out_second"):
        o_got(0, rep_y, "A")
        o_go(3, rep_y, "A", east_dev)
        o_go(4, rep_y, "A", west_dev)
    attend_and_send(1)
    with jax.named_scope("attn_a"):
        gathers[0].second()
    with jax.named_scope("queries"):
        part_got(1)
        place_queries(1)
    attend_and_send(2)
    o_go(15, mine + east, "B", y_dev)
    with jax.named_scope("attn_b"):
        gathers[1].second()
    with jax.named_scope("out_third"):
        o_got(1, mine + west, "A")
        o_go(5, mine + west, "A0", east_dev)
        o_got(2, mine + east, "A")
        o_go(6, mine + east, "A1", west_dev)
    attend_and_send(3)
    with jax.named_scope("out_fourth"):
        o_got(12, mine + far, "B0")
        o_go(16, mine + far, "B0", y_dev)
        o_got(13, mine + far, "B1")
        o_go(17, mine + far, "B1", y_dev)
    with jax.named_scope("attn_c"):
        gathers[0].third()
        gathers[2].second()
    with jax.named_scope("out_fifth"):
        o_got(3, across + west, "A")
        o_go(7, across + west, "A0", east_dev)
        o_got(4, across + east, "A")
        o_go(8, across + east, "A1", west_dev)
    with jax.named_scope("attn_d"):
        gathers[1].third()
        gathers[0].fourth()
        gathers[3].second()
    with jax.named_scope("attn_e"):
        gathers[2].third()
        gathers[1].fourth()
    with jax.named_scope("attn_f"):
        gathers[3].third()
    with jax.named_scope("out_last"):
        out_load.wait()
        o_got(11, rep_y, "B")
        o_got(14, across + west, "B")
        o_got(15, across + east, "B")
        o_got(5, mine + far, "A0")
        o_got(6, mine + far, "A1")
        o_got(16, across + far, "B0")
        o_got(17, across + far, "B1")
        o_got(7, across + far, "A0")
        o_got(8, across + far, "A1")
    out_acc[...] = jnp.zeros_like(out_acc)

    def out_product(first):
        def step(t, carry):
            cols = pl.ds(pl.multiple_of((first + t) * QC, QC), QC)
            out_acc[...] += lax.dot_general(
                gathered[first + t],
                out_rows[:, cols],
                (((1,), (1,)), ((), ())),
                preferred_element_type=jnp.float32,
            )
            return carry

        lax.fori_loop(0, 4, step, 0)

    with jax.named_scope("attn_g"):
        for gather in gathers:
            gather.near()
    with jax.named_scope("out_product"):
        out_product(z * 4)
        out_product(z_down)
        out_product(z_up)
    with jax.named_scope("attn_h"):
        gathers[2].fourth()
        gathers[3].fourth()
        for gather in gathers:
            gather.rest()
    with jax.named_scope("out_product"):
        out_product(z_far)

    residual_load.wait()
    for half in range(2):
        rows = pl.ds(half * HALF_ROWS, HALF_ROWS)
        ended = ends[rows, 0:1]
        picked = jnp.zeros((HALF_ROWS, QC), jnp.float32)
        for step in range(STEPS):
            total = out_acc[pl.ds(half * HALF_TOKENS + step * HALF_ROWS, HALF_ROWS), :]
            total = total + residual[step, rows, :].astype(jnp.float32)
            kept = jnp.where(ended >= step, total, 0.0).astype(jnp.bfloat16)
            decoded[step, rows, :] = kept
            picked = jnp.where(ended == step, kept.astype(jnp.float32), picked)
        at_finish[rows, :] = picked.astype(jnp.bfloat16)

    outgoing[...] = jnp.dot(
        one_hot[...], at_finish[...], preferred_element_type=jnp.float32
    ).astype(jnp.bfloat16)
    for d in range(1, TP):
        to = (tp + d) % TP
        send(
            outgoing.at[pl.ds(pl.multiple_of(to * 16, 16), 16), :],
            stage_one.at[tp],
            one_send,
            one_recv,
            d,
            (rep, to),
        )
    stage_one[tp] = outgoing[pl.ds(pl.multiple_of(tp * 16, 16), 16), :]
    with jax.named_scope("ended_one"):
        for d in range(1, TP):
            receive(stage_one.at[(tp + TP - d) % TP], one_send, one_recv, d)
    for t in range(TP):
        for part in range(QC // HD):
            arrived[:, t * 4 + part, :] = stage_one[t, :, part * HD : (part + 1) * HD].astype(jnp.float32)
    stage_two[0] = arrived[...].astype(jnp.bfloat16)
    for d in range(1, REP):
        to = (rep + d) % REP
        send(
            stage_two.at[0, pl.ds(to * 2, 2)],
            stage_two.at[1, pl.ds(rep * 2, 2)],
            two_send,
            two_recv,
            d,
            (to, tp),
        )
    stage_two[1, pl.ds(rep * 2, 2)] = stage_two[0, pl.ds(rep * 2, 2)]
    with jax.named_scope("ended_two"):
        for d in range(1, REP):
            receive(stage_two.at[1, pl.ds((rep + REP - d) % REP * 2, 2)], two_send, two_recv, d)
    for rank in range(2):
        for r in range(REP):
            arrived[rank * REP + r] = stage_two[1, r * 2 + rank].astype(jnp.float32)
    for part in range(D // HD):
        returned[:, part * HD : (part + 1) * HD] = arrived[:, part, :].astype(jnp.bfloat16)

    with jax.named_scope("sends"):
        for copy in pending:
            copy.wait_send()


def per_device(
    hidden,
    norm_gain,
    q_weight,
    k_weight,
    v_weight,
    o_weight,
    key_cache,
    value_cache,
    cache_len,
    finish,
    owner,
):
    half = HD // 2
    frequency = 500000.0 ** (-(np.arange(HD) % half * 2.0) / HD)
    frequency = jnp.asarray(frequency.reshape(1, HD), jnp.float32)
    hbm = pl.BlockSpec(memory_space=pl.ANY)
    vmem = pl.BlockSpec(memory_space=pltpu.VMEM)
    smem = pl.BlockSpec(memory_space=pltpu.SMEM)
    dma = pltpu.SemaphoreType.DMA
    bf16, f32 = jnp.bfloat16, jnp.float32
    return pl.pallas_call(
        kernel,
        out_shape=(
            jax.ShapeDtypeStruct((STEPS, ROWS, QC), bf16),
            jax.ShapeDtypeStruct((16, D), bf16),
        ),
        in_specs=[hbm, vmem, hbm, hbm, hbm, hbm, hbm, hbm, smem, vmem, vmem, vmem, vmem],
        out_specs=(vmem, vmem),
        scratch_shapes=[
            pltpu.VMEM((SLOTS + 1, CROWS, D), bf16),
            pltpu.VMEM((4, CROWS, BLOCK), bf16),
            pltpu.VMEM((2, 4, TOKENS, BLOCK), bf16),
            pltpu.VMEM((4, BLOCK, WC), bf16),
            pltpu.VMEM((REP * SHARD, D), bf16),
            pltpu.VMEM((ROWS, KEYS, HD), bf16),
            pltpu.VMEM((ROWS, KEYS, HD), bf16),
            pltpu.VMEM((2, TOKENS, WC), f32),
            pltpu.VMEM((2, ROWS, 8, HD), f32),
            pltpu.VMEM((2, TOKENS, WC), bf16),
            pltpu.VMEM((2, TOKENS, HD), bf16),
            pltpu.VMEM((HALF_ROWS, 8, HD), f32),
            pltpu.VMEM((TP, TOKENS, QC), bf16),
            pltpu.VMEM((TOKENS, QC), f32),
            pltpu.VMEM((STEPS, ROWS, QC), bf16),
            pltpu.VMEM((TOKENS, HD), f32),
            pltpu.VMEM((TOKENS, HD), f32),
            pltpu.VMEM((REP * TP * 2, ROWS), bf16),
            pltpu.VMEM((ROWS, ROWS), jnp.int32),
            pltpu.VMEM((KEYS, HD), jnp.int32),
            pltpu.VMEM((ROWS, QC), bf16),
            pltpu.VMEM((256, QC), bf16),
            pltpu.VMEM((TP, 16, QC), bf16),
            pltpu.VMEM((ROWS, 16, HD), f32),
            pltpu.VMEM((2, 16, D // HD, HD), bf16),
            pltpu.VMEM((16, D // HD, HD), f32),
            dma((SLOTS + 1,)),
            dma((6,)),
            dma((3 * TP,)),
            dma((3 * TP,)),
            dma((18,)),
            dma((18,)),
            dma((12,)),
            dma((12,)),
            dma((2,)),
            dma((2,)),
            dma((18,)),
            dma((18,)),
            dma((1,)),
            dma((1,)),
            dma((18 * CHUNKS,)),
            dma((18 * CHUNKS,)),
            dma((TP,)),
            dma((TP,)),
            dma((REP,)),
            dma((REP,)),
        ],
        compiler_params=pltpu.CompilerParams(
            collective_id=0, has_side_effects=True, vmem_limit_bytes=60 * 1024 * 1024
        ),
    )(
        hidden,
        norm_gain.reshape(1, D),
        q_weight,
        k_weight,
        v_weight,
        o_weight,
        key_cache,
        value_cache,
        cache_len,
        cache_len,
        finish,
        owner,
        frequency,
    )


def solution(mesh):
    placed = (
        P(None, "rep", None),
        P(),
        P(("rep", "tp"), None),
        P(("rep", "tp"), None),
        P(("rep", "tp"), None),
        P(("tp", "rep"), None),
        P("rep", "tp", None, None),
        P("rep", "tp", None, None),
        P("rep"),
        P("rep"),
        P("rep", None),
    )
    return jax.shard_map(
        per_device,
        mesh=mesh,
        in_specs=placed,
        out_specs=(P(None, "rep", "tp"), P(("rep", "tp"), None)),
        check_vma=False,
    )
```

time: 215 us -> 153 us (0.71)
  Pallas kernels: 201 us -> 146 us
  other arithmetic: 4.91 us -> 0 us
    pallas_call x1, Pallas kernels: 201 us -> 146 us  [per_device(): pl.pallas_call(kernel, out_shape=(jax.ShapeDtypeStruct((STEPS, ROWS, QC),...]
    unnamed x2 -> x3, local copies, waits for them, and re-layouts: 3.54 us -> 4.93 us
where the time goes in v3:
time: 153 us
  Pallas kernels  146 us (95%)
  local copies, waits for them, and re-layouts  6.28 us (4%)
    pallas_call x1, Pallas kernels, per_device(): pl.pallas_call(kernel, out_shape=(jax.ShapeDtypeStruct((STEPS, ROWS, QC),...  146 us
    unnamed x3, local copies, waits for them, and re-layouts  4.93 us

profile of v3, /device:TPU:1, one launch (start us, length us, event | category | flops | bytes accessed | tf_op | source)
XLA Modules:
  0.0 152.5 jit_solution(1198962700353626593)
XLA Ops:
  0.6 1.4 reshape.7.gain
  2.0 1.4 copy.14.owner
  3.4 145.6 %shard_map.131 = (bf16[4,128,512]{2,1,0:T(8,128)(2,1)}, bf16[16,8192]{1,0:T(8,128)(2,1)}) custom-call(bf16[4,128,8192]{2,1,0:T(8,128)(2,1)} %hidden.1, bf16[1,8192]{1,0:T(2,128)(2,1)} %reshape.7.gain, bf16[64,8192]{1,0:T(8,128)(2,1)} %q_weight.1, bf16[64,1024]{1,0:T(8,128)(2,1)} %k_weight.1, bf16[64,1024]{1,0:T(8,128)(2,1)} %v_weight.1, ...), custom_call_target="tpu_custom_call" | custom-call | tf_op jit(solution)/shard_map/pallas_call | solution.py:783
  149.0 1.9 %copy.17 = bf16[4,128,512]{2,1,0:T(8,128)(2,1)} copy(bf16[4,128,512]{2,1,0:T(8,128)(2,1)} %get-tuple-element.4) | data formatting | bytes 1048576
  150.9 1.7 %copy.18 = bf16[16,8192]{1,0:T(8,128)(2,1)} copy(bf16[16,8192]{1,0:T(8,128)(2,1)} %get-tuple-element.5) | data formatting | bytes 524288

commit v4 on v3

--- a/solution.py
+++ b/solution.py
@@ -22,6 +22,7 @@
 BLOCK = TP * SHARD
 TOKENS = STEPS * ROWS
 CHUNKS = 4
+Z_FIRST = ()
 SLOTS = 4
 CROWS = ROWS // CHUNKS
 HALF_ROWS = ROWS // 2
@@ -29,7 +30,6 @@
 EPS = 1e-05
 
 STAGES = ((0, 384), (384, 256))
-OUT_CUT = 5120
 
 
 def kernel(
@@ -49,6 +49,7 @@
     decoded,
     returned,
     staged,
+    gain_row,
     shared,
     normed,
     weights,
@@ -60,8 +61,10 @@
     partial,
     pair,
     attn_rows,
+    away,
     gathered,
     out_acc,
+    out_part,
     residual,
     cosine,
     sine,
@@ -76,6 +79,7 @@
     arrived,
     load_sem,
     local_sem,
+    out_sem,
     a2a_send,
     a2a_recv,
     norm_send,
@@ -88,8 +92,12 @@
     out_recv,
     pair_send,
     pair_recv,
+    away_send,
+    away_recv,
     attn_send,
     attn_recv,
+    last_send,
+    last_recv,
     one_send,
     one_recv,
     two_send,
@@ -98,16 +106,14 @@
     rep = lax.axis_index("rep")
     tp = lax.axis_index("tp")
     y, x = rep // 4, rep % 4
-    across = (1 - y) * 4
-    mine = y * 4
     east, west, far = (x + 1) % 4, (x + 3) % 4, (x + 2) % 4
-    rep_east, rep_west, rep_y = mine + east, mine + west, across + x
+    rep_east, rep_west, rep_y = y * 4 + east, y * 4 + west, (1 - y) * 4 + x
     z, low = tp // 4, tp % 4
     core_peer = tp + 1 - 2 * (tp % 2)
     hi_peer = tp + 2 - 4 * ((tp // 2) % 2)
     pending = []
 
-    def send(src, dst, sends, recvs, k, to):
+    def send(src, dst, sends, recvs, k, to, start=True):
         copy = pltpu.make_async_remote_copy(
             src_ref=src,
             dst_ref=dst,
@@ -116,8 +122,10 @@
             device_id=to,
             device_id_type=MESH,
         )
-        copy.start()
+        if start:
+            copy.start()
         pending.append(copy)
+        return copy
 
     def receive(region, sends, recvs, k):
         pltpu.make_async_remote_copy(
@@ -138,6 +146,9 @@
         pl.semaphore_signal(
             barrier, inc=1, device_id=((rep + d) % REP, tp), device_id_type=MESH
         )
+    both_peer = hi_peer + 1 - 2 * (tp % 2)
+    for peer in (core_peer, both_peer):
+        pl.semaphore_signal(barrier, inc=1, device_id=(rep_y, peer), device_id_type=MESH)
     key_load = pltpu.make_async_copy(
         key_cache.at[:, 0], keys.at[:, pl.ds(0, CACHE), :], local_sem.at[0]
     )
@@ -157,25 +168,26 @@
     k_load = pltpu.make_async_copy(k_weight.at[:, kv_cols], my_kv, local_sem.at[4])
     v_load = pltpu.make_async_copy(v_weight.at[:, kv_cols], my_kv, local_sem.at[4])
 
-    def out_block(r, part):
-        start, size = {
-            "A": (0, OUT_CUT),
-            "A0": (0, OUT_CUT // 2),
-            "A1": (OUT_CUT // 2, OUT_CUT // 2),
-            "B": (OUT_CUT, D - OUT_CUT),
-            "B0": (OUT_CUT, (D - OUT_CUT) // 2),
-            "B1": (OUT_CUT + (D - OUT_CUT) // 2, (D - OUT_CUT) // 2),
-            "all": (0, D),
-        }[part]
-        return out_rows.at[
-            pl.ds(pl.multiple_of(r * SHARD, SHARD), SHARD), pl.ds(start, size)
-        ]
-
-    out_load = pltpu.make_async_copy(o_weight, out_block(rep, "all"), local_sem.at[5])
+    def out_block(side, at, part="all"):
+        start, size = {"all": (0, D // 2), "0": (0, D // 4), "1": (D // 4, D // 4)}[part]
+        rows = pl.ds(pl.multiple_of((side * 4 + at) * SHARD, SHARD), SHARD)
+        return out_rows.at[rows, pl.ds(start, size)]
+
+    def out_piece(side, j):
+        rows = pl.ds(pl.multiple_of((side * 4 + x) * SHARD, SHARD), SHARD)
+        return out_rows.at[rows, pl.ds(j * QC, QC)]
+
+    def out_source(core, j):
+        return o_weight.at[:, pl.ds(pl.multiple_of((j * 2 + core) * QC, QC), QC)]
+
+    out_loads = [
+        pltpu.make_async_copy(out_source(y, j), out_piece(y, j), out_sem.at[j]) for j in range(TP // 2)
+    ]
     q_load.start()
     pl.when(tp % 2 == 0)(k_load.start)
     pl.when(tp % 2 == 1)(v_load.start)
-    out_load.start()
+    for load in out_loads:
+        load.start()
 
     def hidden_load(step, slot):
         return pltpu.make_async_copy(
@@ -185,6 +197,7 @@
         )
 
     hidden_load(tp, SLOTS).start()
+    gain_row[...] = gain[...].astype(jnp.float32).reshape(1, D)
     for step in range(SLOTS - 1):
         hidden_load(step, step).start()
     def norm_rows(slot, half, part, store):
@@ -195,7 +208,7 @@
         for b in range(4):
             cols = pl.ds(pl.multiple_of(half * (D // 2) + b * BLOCK, BLOCK), BLOCK)
             block = staged[slot, part_rows, cols].astype(jnp.float32)
-            block = block * scale * gain[:, cols].astype(jnp.float32)
+            block = block * scale * gain_row[:, cols]
             store(b, block.astype(jnp.bfloat16))
 
     def norm_step(step, carry):
@@ -236,8 +249,10 @@
         rows = pl.ds(pl.multiple_of(t * CROWS, CROWS), CROWS)
         return normed.at[1, pl.ds(start, size), rows, :]
 
+    with jax.named_scope("norm"):
+        lax.fori_loop(0, 4, norm_step, 0)
     with jax.named_scope("greet"):
-        pl.semaphore_wait(barrier, TP - 1 + REP - 1)
+        pl.semaphore_wait(barrier, TP - 1 + REP + 1)
 
     q_parts = ((0, STAGES[0][1] - HD), (STAGES[0][1] - HD, STAGES[1][1]))
     def a2a_go(stage):
@@ -283,15 +298,30 @@
 
     east_dev, west_dev, y_dev = (rep_east, tp), (rep_west, tp), (rep_y, tp)
 
-    def o_go(k, r, part, to, src=None):
-        dst = out_block(r, part)
-        send(dst if src is None else src, dst, out_send, out_recv, k, to)
-
-    def o_got(k, r, part):
-        receive(out_block(r, part), out_send, out_recv, k)
-
-    o_a = o_weight.at[:, pl.ds(0, OUT_CUT)]
-    o_b = o_weight.at[:, pl.ds(OUT_CUT, D - OUT_CUT)]
+    def o_swap():
+        for j in range(TP // 2):
+            send(out_source(1 - y, j), out_piece(y, j), out_send, out_recv, j, y_dev)
+
+    def o_swapped():
+        for j in range(TP // 2):
+            receive(out_piece(1 - y, j), out_send, out_recv, j)
+
+    def o_own(side, base):
+        block = out_block(side, x)
+        send(block, block, out_send, out_recv, base, east_dev)
+        send(block, block, out_send, out_recv, base + 1, west_dev)
+
+    def o_on(side, base):
+        receive(out_block(side, west), out_send, out_recv, base)
+        block = out_block(side, west, "0")
+        send(block, block, out_send, out_recv, base + 2, east_dev)
+        receive(out_block(side, east), out_send, out_recv, base + 1)
+        block = out_block(side, east, "1")
+        send(block, block, out_send, out_recv, base + 3, west_dev)
+
+    def o_far(side, base):
+        receive(out_block(side, far, "0"), out_send, out_recv, base + 2)
+        receive(out_block(side, far, "1"), out_send, out_recv, base + 3)
 
     z_up, z_down, z_far = (z + 1) % 4 * 4, (z + 3) % 4 * 4, (z + 2) % 4 * 4
     low_hi, low_core = hi_peer % 4, core_peer % 4
@@ -303,18 +333,20 @@
         def __init__(self, block, sends, recvs, base):
             self.block, self.sends, self.recvs, self.base = block, sends, recvs, base
 
-        def go(self, k, t, to, part="all"):
+        def go(self, k, t, to, part="all", start=True):
             block = self.block(t, part)
-            send(block, block, self.sends, self.recvs, self.base + k, to)
+            return send(block, block, self.sends, self.recvs, self.base + k, to, start)
 
         def got(self, k, t, part="all"):
             receive(self.block(t, part), self.sends, self.recvs, self.base + k)
 
-        def first(self):
-            self.go(0, tp, hi_dev)
-            self.go(1, tp, up_dev)
-            self.go(2, tp, down_dev)
-            self.go(3, tp, core_dev)
+        def first(self, start=True):
+            return [
+                self.go(0, tp, hi_dev, start=start),
+                self.go(1, tp, up_dev, start=start),
+                self.go(2, tp, down_dev, start=start),
+                self.go(3, tp, core_dev, start=start),
+            ]
 
         def second(self):
             self.got(0, hi_peer)
@@ -356,12 +388,41 @@
             self.got(15, z_far + low_core)
             self.got(16, z_far + low_both)
 
+    class TpGatherZ(TpGather):
+        def second(self):
+            self.got(1, z_down + low)
+            self.go(7, z_down + low, up_dev, "0")
+            self.go(4, z_down + low, hi_dev)
+            self.got(2, z_up + low)
+            self.go(8, z_up + low, down_dev, "1")
+            self.go(5, z_up + low, hi_dev)
+            self.got(0, hi_peer)
+            self.go(6, hi_peer, core_dev)
+            self.go(9, z_down + low, core_dev)
+            self.go(10, z_up + low, core_dev)
+
+        def third(self):
+            self.got(7, z_far + low, "0")
+            self.got(8, z_far + low, "1")
+            self.go(11, z_far + low, hi_dev)
+            self.go(15, z_far + low, core_dev)
+            self.got(4, z_down + low_hi)
+            self.go(13, z_down + low_hi, core_dev)
+            self.got(5, z_up + low_hi)
+            self.go(14, z_up + low_hi, core_dev)
+
+        def fourth(self):
+            self.got(11, z_far + low_hi)
+            self.go(16, z_far + low_hi, core_dev)
+
     norm_gather = TpGather(norm_block, norm_send, norm_recv, 0)
     send(shared, norm_block(tp, "all"), norm_send, norm_recv, 17, y_dev)
     a2a_go(0)
-    a2a_go(1)
-    o_go(9, rep, "B", east_dev, o_b)
-    o_go(10, rep, "B", west_dev, o_b)
+    for load in out_loads:
+        load.wait()
+    o_own(y, 8)
+
+    out_acc[...] = jnp.zeros_like(out_acc)
 
     with jax.named_scope("tables"):
         square = (ROWS, ROWS)
@@ -375,8 +436,8 @@
         finish_cols = jnp.broadcast_to(finish_row[...].reshape(1, ROWS), square)
         finish_rows = flip(finish_cols)
         ends[...] = finish_rows
-        owner_rows = jnp.broadcast_to(owner[...], square)
-        owner_cols = flip(owner_rows)
+        owner_cols = jnp.broadcast_to(owner[...].reshape(1, ROWS), square)
+        owner_rows = flip(owner_cols)
         sign = jnp.where(cols_at < HD // 2, -1.0, 1.0)
         for step in range(STEPS):
             angles = (lens_col + float(step)) * frequency[...]
@@ -443,17 +504,29 @@
 
         lax.fori_loop(0, TOKENS // 256, tile, 0)
 
-    def part_block(which, stage):
+    def part_block(which, stage, half):
         start, size = STAGES[stage]
-        return partial.at[which, :, pl.ds(start, size)]
+        return partial.at[which, :, pl.ds(half * HALF_ROWS, HALF_ROWS), pl.ds(start, size)]
 
     def part_go(stage):
         start, size = STAGES[stage]
-        partial[0, :, start : start + size] = acc[1, :, start : start + size].astype(jnp.bfloat16)
-        send(part_block(0, stage), part_block(1, stage), part_send, part_recv, stage, y_dev)
-
-    def part_got(stage):
-        receive(part_block(1, stage), part_send, part_recv, stage)
+        for half in range(2):
+            for step in range(STEPS):
+                rows = pl.ds(step * ROWS + half * HALF_ROWS, HALF_ROWS)
+                partial[0, step, pl.ds(half * HALF_ROWS, HALF_ROWS), start : start + size] = acc[
+                    1, rows, start : start + size
+                ].astype(jnp.bfloat16)
+            send(
+                part_block(0, stage, half),
+                part_block(1, stage, half),
+                part_send,
+                part_recv,
+                stage * 2 + half,
+                y_dev,
+            )
+
+    def part_got(stage, half):
+        receive(part_block(1, stage, half), part_send, part_recv, stage * 2 + half)
 
     with jax.named_scope("norm_over_y"):
         receive(norm_block(tp, "all"), norm_send, norm_recv, 17)
@@ -463,26 +536,24 @@
         k_load.wait()
         a2a_got(0)
         ring_own(0)
-        o_go(0, rep, "A", y_dev, o_a)
+        a2a_go(1)
     with jax.named_scope("norm"):
-        lax.fori_loop(0, 8, norm_step, 0)
+        lax.fori_loop(4, 16, norm_step, 0)
     with jax.named_scope("norm_second"):
         norm_gather.second()
     with jax.named_scope("ring_on_0"):
         ring_on(0)
-    with jax.named_scope("norm"):
-        lax.fori_loop(8, 16, norm_step, 0)
-    with jax.named_scope("ring_near_0"):
-        ring_near(0)
-        a2a_got(1)
-        ring_own(1)
-    with jax.named_scope("norm_third"):
-        norm_gather.third()
+        o_swap()
     key_load.start()
     value_load.start()
     residual_load.start()
+    with jax.named_scope("norm_third"):
+        norm_gather.third()
     with jax.named_scope("project"):
         project(0, 0, x, True)
+    with jax.named_scope("ring_near_0"):
+        ring_near(0)
+    with jax.named_scope("project"):
         project(0, 0, west)
         project(0, 0, east)
     with jax.named_scope("norm_last"):
@@ -495,69 +566,73 @@
         project(0, 1, east)
     with jax.named_scope("ring_far_0"):
         ring_far(0)
+        a2a_got(1)
+        ring_own(1)
         project(0, 1, far)
         part_go(0)
-        o_go(11, rep, "B", y_dev, o_b)
-        o_got(9, mine + west, "B")
-        o_got(10, mine + east, "B")
         project(0, 0, far)
-    with jax.named_scope("ring_on_1"):
-        ring_on(1)
     with jax.named_scope("project"):
         project(1, 0, x, True)
         project(1, 1, x, True)
-    with jax.named_scope("out_first"):
-        o_go(1, rep, "A", east_dev, o_a)
-        o_go(2, rep, "A", west_dev, o_a)
-        o_go(12, mine + west, "B0", east_dev)
-        o_go(13, mine + east, "B1", west_dev)
 
     def rotate(block, rows):
         return block * cosine[rows, :] + pltpu.roll(block, HD // 2, 1) * sine[rows, :]
 
-    def total(step, start):
-        rows = pl.ds(step * ROWS, ROWS)
+    def total(step, half, start):
+        rows = pl.ds(step * ROWS + half * HALF_ROWS, HALF_ROWS)
         cols = slice(start, start + HD)
-        return acc[0, rows, cols] + partial[1, rows, cols].astype(jnp.float32)
-
-    def place_queries(stage):
+        there = partial[1, step, pl.ds(half * HALF_ROWS, HALF_ROWS), cols]
+        return acc[0, rows, cols] + there.astype(jnp.float32)
+
+    def place_queries(stage, half):
         for step in range(STEPS):
-            rows = pl.ds(step * ROWS, ROWS)
+            rows = pl.ds(step * ROWS + half * HALF_ROWS, HALF_ROWS)
             for h in range(2):
                 start = HD + (stage * 2 + h) * HD
-                queries[stage, :, step * 2 + h, :] = rotate(total(step, start), rows)
+                queries[stage, pl.ds(half * HALF_ROWS, HALF_ROWS), step * 2 + h, :] = rotate(
+                    total(step, half, start), rows
+                )
 
     is_key = tp % 2 == 0
+
+    def pair_block(which, half):
+        return pair.at[which, :, pl.ds(half * HALF_ROWS, HALF_ROWS), :]
+
+    def pair_go(half):
+        part_got(0, half)
+        for step in range(STEPS):
+            rows = pl.ds(step * ROWS + half * HALF_ROWS, HALF_ROWS)
+            block = total(step, half, 0)
+            pair[0, step, pl.ds(half * HALF_ROWS, HALF_ROWS), :] = jnp.where(
+                is_key, rotate(block, rows), block
+            ).astype(jnp.bfloat16)
+        send(pair_block(0, half), pair_block(1, half), pair_send, pair_recv, half, core_dev)
+        place_queries(0, half)
+
+    def pair_got(half):
+        receive(pair_block(1, half), pair_send, pair_recv, half)
+        half_rows = pl.ds(half * HALF_ROWS, HALF_ROWS)
+        for place, target in ((0, keys), (1, values)):
+            spread[...] = jnp.zeros((HALF_ROWS, 16, HD), jnp.float32)
+            slot = (tp + place) % 2
+            for step in range(STEPS):
+                spread[:, step, :] = pair[slot, step, half_rows, :].astype(jnp.float32)
+            target[half_rows, pl.ds(CACHE, 16), :] = spread[...].astype(jnp.bfloat16)
+
     with jax.named_scope("keys"):
-        part_got(0)
-        for step in range(STEPS):
-            rows = pl.ds(step * ROWS, ROWS)
-            block = total(step, 0)
-            pair[0, rows, :] = jnp.where(is_key, rotate(block, rows), block).astype(jnp.bfloat16)
-        send(pair.at[0], pair.at[1], pair_send, pair_recv, 0, core_dev)
-        place_queries(0)
-    with jax.named_scope("ring_near_1"):
-        ring_near(1)
-    with jax.named_scope("project"):
-        project(1, 1, west)
-        project(1, 1, east)
-        project(1, 0, west)
-        project(1, 0, east)
-    receive(pair.at[1], pair_send, pair_recv, 0)
-    key_load.wait()
-    value_load.wait()
-    zeros = jnp.zeros((ROWS, 16, HD), jnp.float32)
-    for place, target in ((0, keys), (1, values)):
-        spread[...] = zeros
-        slot = (tp + place) % 2
-        for step in range(STEPS):
-            spread[:, step, :] = pair[slot, pl.ds(step * ROWS, ROWS), :].astype(jnp.float32)
-        target[:, pl.ds(CACHE, 16), :] = spread[...].astype(jnp.bfloat16)
-
+        pair_go(0)
+    with jax.named_scope("ring_on_1"):
+        ring_on(1)
+    with jax.named_scope("keys"):
+        key_load.wait()
+        value_load.wait()
+        pair_got(0)
+
+    stays, goes = tp % 2 == y, tp % 2 != y
     row_of = lax.broadcasted_iota(jnp.int32, (KEYS, HD), 1) // 8
     score_scale = 1.0 / (float(HD) ** 0.5)
 
-    def attend(stage, half):
+    def attend(stage, half, between):
         def rows_of_16(it, carry):
             first = half * HALF_ROWS + it * 16
             query = queries[stage, pl.ds(first, 16)].reshape(16 * 8, HD).astype(jnp.bfloat16)
@@ -582,14 +657,20 @@
                 )
             return carry
 
-        lax.fori_loop(0, HALF_ROWS // 16, rows_of_16, 0)
-        for step in range(STEPS):
-            for h in range(2):
-                gathered[
-                    tp,
-                    pl.ds(half * HALF_TOKENS + step * HALF_ROWS, HALF_ROWS),
-                    pl.ds((stage * 2 + h) * HD, HD),
-                ] = attn_rows[:, step * 2 + h, :].astype(jnp.bfloat16)
+        lax.fori_loop(0, HALF_ROWS // 32, rows_of_16, 0)
+        between()
+        lax.fori_loop(HALF_ROWS // 32, HALF_ROWS // 16, rows_of_16, 0)
+
+        def place(target):
+            for step in range(STEPS):
+                for h in range(2):
+                    target[
+                        pl.ds(half * HALF_TOKENS + step * HALF_ROWS, HALF_ROWS),
+                        pl.ds((stage * 2 + h) * HD, HD),
+                    ] = attn_rows[:, step * 2 + h, :].astype(jnp.bfloat16)
+
+        pl.when(stays)(lambda: place(gathered.at[tp]))
+        pl.when(goes)(lambda: place(away))
 
     def attn_block(t, chunk, part="all"):
         size = HALF_TOKENS // 2
@@ -599,114 +680,167 @@
 
     PER = 18
     gathers = [
-        TpGather(
+        (TpGatherZ if chunk in Z_FIRST else TpGather)(
             lambda t, part, chunk=chunk: attn_block(t, chunk, part), attn_send, attn_recv, chunk * PER
         )
         for chunk in range(CHUNKS)
     ]
 
-    def attend_and_send(chunk):
+    def away_copy(chunk, to, sends, recvs, k):
+        rows = pl.ds(chunk % 2 * HALF_TOKENS, HALF_TOKENS)
+        return pltpu.make_async_remote_copy(
+            src_ref=away.at[rows, pl.ds(chunk // 2 * 2 * HD, 2 * HD)],
+            dst_ref=attn_block(core_peer, chunk),
+            send_sem=sends.at[k],
+            recv_sem=recvs.at[k],
+            device_id=(rep_y, to),
+            device_id_type=MESH,
+        )
+
+    own_sends = {}
+
+    def attend_and_send(chunk, between=lambda: None):
         with jax.named_scope("attend"):
-            attend(chunk // 2, chunk % 2)
-        gathers[chunk].first()
+            attend(chunk // 2, chunk % 2, between)
+        own_sends[chunk] = gathers[chunk].first(start=False)
+
+        @pl.when(stays)
+        def _():
+            for copy in own_sends[chunk]:
+                copy.start()
+
+        @pl.when(goes)
+        def _():
+            away_copy(chunk, core_peer, away_send, away_recv, chunk).start()
+            away_copy(chunk, both_peer, attn_send, attn_recv, chunk * PER).start()
+
+    def first_of_other(chunk):
+        @pl.when(goes)
+        def _():
+            receive(attn_block(tp, chunk), away_send, away_recv, chunk)
+            for copy in own_sends[chunk][1:]:
+                copy.start()
 
     attend_and_send(0)
+    with jax.named_scope("keys"):
+        pair_go(1)
+    with jax.named_scope("ring_near_1"):
+        ring_near(1)
+        project(1, 1, west)
+        project(1, 1, east)
+        project(1, 0, west)
+        project(1, 0, east)
     with jax.named_scope("ring_far_1"):
         ring_far(1)
+        o_on(y, 8)
+        o_swapped()
+        o_own(1 - y, 12)
         project(1, 1, far)
         part_go(1)
         project(1, 0, far)
-        o_go(14, mine + west, "B", y_dev)
-    with jax.named_scope("out_second"):
-        o_got(0, rep_y, "A")
-        o_go(3, rep_y, "A", east_dev)
-        o_go(4, rep_y, "A", west_dev)
+    with jax.named_scope("attn_0"):
+        first_of_other(0)
+    with jax.named_scope("keys"):
+        pair_got(1)
     attend_and_send(1)
-    with jax.named_scope("attn_a"):
+    with jax.named_scope("attn_1"):
         gathers[0].second()
     with jax.named_scope("queries"):
-        part_got(1)
-        place_queries(1)
-    attend_and_send(2)
-    o_go(15, mine + east, "B", y_dev)
-    with jax.named_scope("attn_b"):
-        gathers[1].second()
-    with jax.named_scope("out_third"):
-        o_got(1, mine + west, "A")
-        o_go(5, mine + west, "A0", east_dev)
-        o_got(2, mine + east, "A")
-        o_go(6, mine + east, "A1", west_dev)
-    attend_and_send(3)
-    with jax.named_scope("out_fourth"):
-        o_got(12, mine + far, "B0")
-        o_go(16, mine + far, "B0", y_dev)
-        o_got(13, mine + far, "B1")
-        o_go(17, mine + far, "B1", y_dev)
-    with jax.named_scope("attn_c"):
-        gathers[0].third()
+        for half in range(2):
+            part_got(1, half)
+            place_queries(1, half)
+
+    def between_2():
+        with jax.named_scope("attn_2"):
+            first_of_other(1)
+
+    attend_and_send(2, between_2)
+
+    def between_3():
+        with jax.named_scope("attn_3"):
+            gathers[1].second()
+            gathers[0].third()
+
+    attend_and_send(3, between_3)
+    with jax.named_scope("attn_4"):
+        first_of_other(2)
         gathers[2].second()
-    with jax.named_scope("out_fifth"):
-        o_got(3, across + west, "A")
-        o_go(7, across + west, "A0", east_dev)
-        o_got(4, across + east, "A")
-        o_go(8, across + east, "A1", west_dev)
-    with jax.named_scope("attn_d"):
+        first_of_other(3)
+        o_on(1 - y, 12)
         gathers[1].third()
+        gathers[3].second()
+    with jax.named_scope("attn_5"):
         gathers[0].fourth()
-        gathers[3].second()
-    with jax.named_scope("attn_e"):
         gathers[2].third()
         gathers[1].fourth()
-    with jax.named_scope("attn_f"):
-        gathers[3].third()
     with jax.named_scope("out_last"):
-        out_load.wait()
-        o_got(11, rep_y, "B")
-        o_got(14, across + west, "B")
-        o_got(15, across + east, "B")
-        o_got(5, mine + far, "A0")
-        o_got(6, mine + far, "A1")
-        o_got(16, across + far, "B0")
-        o_got(17, across + far, "B1")
-        o_got(7, across + far, "A0")
-        o_got(8, across + far, "A1")
-    out_acc[...] = jnp.zeros_like(out_acc)
-
-    def out_product(first):
-        def step(t, carry):
-            cols = pl.ds(pl.multiple_of((first + t) * QC, QC), QC)
-            out_acc[...] += lax.dot_general(
-                gathered[first + t],
+        o_far(y, 8)
+        o_far(1 - y, 12)
+
+    def out_product(half, first):
+        rows = pl.ds(half * HALF_TOKENS, HALF_TOKENS)
+
+        def step(h, carry):
+            t = first + h * 2
+            cols = pl.ds(pl.multiple_of((first // 2 + h) * QC, QC), QC)
+            part = lax.dot_general(
+                gathered[pl.ds(t, 2), rows, :].reshape(2 * HALF_TOKENS, QC),
                 out_rows[:, cols],
                 (((1,), (1,)), ((), ())),
                 preferred_element_type=jnp.float32,
             )
+            out_acc[:, rows, :] += part.reshape(2, HALF_TOKENS, QC)
             return carry
 
-        lax.fori_loop(0, 4, step, 0)
-
-    with jax.named_scope("attn_g"):
-        for gather in gathers:
-            gather.near()
+        lax.fori_loop(0, 2, step, 0)
+
+    def out_part_go(half):
+        rows = pl.ds(half * HALF_TOKENS, HALF_TOKENS)
+        out_part[0, rows, :] = out_acc[1 - y, rows, :].astype(jnp.bfloat16)
+        send(out_part.at[0, rows], out_part.at[1, rows], last_send, last_recv, half, y_dev)
+
+    with jax.named_scope("attn_6"):
+        gathers[0].near()
+        gathers[2].near()
     with jax.named_scope("out_product"):
-        out_product(z * 4)
-        out_product(z_down)
-        out_product(z_up)
-    with jax.named_scope("attn_h"):
+        out_product(0, z * 4)
+        out_product(0, z_down)
+        out_product(0, z_up)
+    with jax.named_scope("attn_7"):
         gathers[2].fourth()
+        gathers[0].rest()
+        gathers[2].rest()
+    with jax.named_scope("out_product"):
+        out_product(0, z_far)
+        out_part_go(0)
+    with jax.named_scope("attn_7b"):
+        gathers[3].third()
+    with jax.named_scope("attn_8"):
+        gathers[1].near()
+        gathers[3].near()
+    with jax.named_scope("out_product"):
+        out_product(1, z * 4)
+        out_product(1, z_down)
+        out_product(1, z_up)
+    with jax.named_scope("attn_9"):
         gathers[3].fourth()
-        for gather in gathers:
-            gather.rest()
+        gathers[1].rest()
+        gathers[3].rest()
     with jax.named_scope("out_product"):
-        out_product(z_far)
+        out_product(1, z_far)
+        out_part_go(1)
 
     residual_load.wait()
     for half in range(2):
         rows = pl.ds(half * HALF_ROWS, HALF_ROWS)
         ended = ends[rows, 0:1]
         picked = jnp.zeros((HALF_ROWS, QC), jnp.float32)
+        half_tokens = pl.ds(half * HALF_TOKENS, HALF_TOKENS)
+        with jax.named_scope("out_part"):
+            receive(out_part.at[1, half_tokens], last_send, last_recv, half)
         for step in range(STEPS):
-            total = out_acc[pl.ds(half * HALF_TOKENS + step * HALF_ROWS, HALF_ROWS), :]
+            tokens = pl.ds(half * HALF_TOKENS + step * HALF_ROWS, HALF_ROWS)
+            total = out_acc[y, tokens, :] + out_part[1, tokens, :].astype(jnp.float32)
             total = total + residual[step, rows, :].astype(jnp.float32)
             kept = jnp.where(ended >= step, total, 0.0).astype(jnp.bfloat16)
             decoded[step, rows, :] = kept
@@ -758,6 +892,11 @@
         for copy in pending:
             copy.wait_send()
 
+        @pl.when(goes)
+        def _():
+            for chunk in range(CHUNKS):
+                away_copy(chunk, core_peer, away_send, away_recv, chunk).wait_send()
+
 
 def per_device(
     hidden,
@@ -790,19 +929,22 @@
         out_specs=(vmem, vmem),
         scratch_shapes=[
             pltpu.VMEM((SLOTS + 1, CROWS, D), bf16),
+            pltpu.VMEM((1, D), f32),
             pltpu.VMEM((4, CROWS, BLOCK), bf16),
             pltpu.VMEM((2, 4, TOKENS, BLOCK), bf16),
             pltpu.VMEM((4, BLOCK, WC), bf16),
-            pltpu.VMEM((REP * SHARD, D), bf16),
+            pltpu.VMEM((REP * SHARD, D // 2), bf16),
             pltpu.VMEM((ROWS, KEYS, HD), bf16),
             pltpu.VMEM((ROWS, KEYS, HD), bf16),
             pltpu.VMEM((2, TOKENS, WC), f32),
             pltpu.VMEM((2, ROWS, 8, HD), f32),
-            pltpu.VMEM((2, TOKENS, WC), bf16),
-            pltpu.VMEM((2, TOKENS, HD), bf16),
+            pltpu.VMEM((2, STEPS, ROWS, WC), bf16),
+            pltpu.VMEM((2, STEPS, ROWS, HD), bf16),
             pltpu.VMEM((HALF_ROWS, 8, HD), f32),
+            pltpu.VMEM((TOKENS, QC), bf16),
             pltpu.VMEM((TP, TOKENS, QC), bf16),
-            pltpu.VMEM((TOKENS, QC), f32),
+            pltpu.VMEM((2, TOKENS, QC), f32),
+            pltpu.VMEM((2, TOKENS, QC), bf16),
             pltpu.VMEM((STEPS, ROWS, QC), bf16),
             pltpu.VMEM((TOKENS, HD), f32),
             pltpu.VMEM((TOKENS, HD), f32),
@@ -812,25 +954,30 @@
             pltpu.VMEM((ROWS, QC), bf16),
             pltpu.VMEM((256, QC), bf16),
             pltpu.VMEM((TP, 16, QC), bf16),
-            pltpu.VMEM((ROWS, 16, HD), f32),
+            pltpu.VMEM((HALF_ROWS, 16, HD), f32),
             pltpu.VMEM((2, 16, D // HD, HD), bf16),
             pltpu.VMEM((16, D // HD, HD), f32),
             dma((SLOTS + 1,)),
             dma((6,)),
+            dma((TP // 2,)),
             dma((3 * TP,)),
             dma((3 * TP,)),
             dma((18,)),
             dma((18,)),
             dma((12,)),
             dma((12,)),
+            dma((4,)),
+            dma((4,)),
+            dma((18,)),
+            dma((18,)),
             dma((2,)),
             dma((2,)),
-            dma((18,)),
-            dma((18,)),
-            dma((1,)),
-            dma((1,)),
+            dma((CHUNKS,)),
+            dma((CHUNKS,)),
             dma((18 * CHUNKS,)),
             dma((18 * CHUNKS,)),
+            dma((2,)),
+            dma((2,)),
             dma((TP,)),
             dma((TP,)),
             dma((REP,)),
@@ -841,7 +988,7 @@
         ),
     )(
         hidden,
-        norm_gain.reshape(1, D),
+        norm_gain,
         q_weight,
         k_weight,
         v_weight,
@@ -851,7 +998,7 @@
         cache_len,
         cache_len,
         finish,
-        owner,
+        owner.reshape(ROWS),
         frequency,
     )
 

time: 153 us -> 150 us (0.980)
  local copies, waits for them, and re-layouts: 6.28 us -> 3.54 us
    unnamed x3 -> x2, local copies, waits for them, and re-layouts: 4.93 us -> 3.54 us
where the time goes in v4:
time: 150 us
  Pallas kernels  145 us (97%)
  local copies, waits for them, and re-layouts  3.54 us (2%)
    pallas_call x1, Pallas kernels, per_device(): pl.pallas_call(kernel, out_shape=(jax.ShapeDtypeStruct((STEPS, ROWS, QC),...  145 us
    unnamed x2, local copies, waits for them, and re-layouts  3.54 us

profile of v4, /device:TPU:1, one launch (start us, length us, event | category | flops | bytes accessed | tf_op | source)
XLA Modules:
  0.0 149.6 jit_solution(1455941868068746191)
XLA Ops:
  0.6 145.5 %shard_map.131 = (bf16[4,128,512]{2,1,0:T(8,128)(2,1)}, bf16[16,8192]{1,0:T(8,128)(2,1)}) custom-call(bf16[4,128,8192]{2,1,0:T(8,128)(2,1)} %hidden.1, bf16[8192]{0:T(1024)(128)(2,1)} %gain.1, bf16[64,8192]{1,0:T(8,128)(2,1)} %q_weight.1, bf16[64,1024]{1,0:T(8,128)(2,1)} %k_weight.1, bf16[64,1024]{1,0:T(8,128)(2,1)} %v_weight.1, bf16[64,8192]{1,0:T(8,128)(2,1)} %o_weight.1, ...), custom_call_target="tpu_custom_call" | custom-call | tf_op jit(solution)/shard_map/pallas_call | solution.py:922
  146.1 1.9 %copy.16 = bf16[4,128,512]{2,1,0:T(8,128)(2,1)} copy(bf16[4,128,512]{2,1,0:T(8,128)(2,1)} %get-tuple-element.4) | data formatting | bytes 1048576
  148.0 1.7 %copy.17 = bf16[16,8192]{1,0:T(8,128)(2,1)} copy(bf16[16,8192]{1,0:T(8,128)(2,1)} %get-tuple-element.5) | data formatting | bytes 524288

commit v5 on v4

--- a/solution.py
+++ b/solution.py
@@ -22,7 +22,7 @@
 BLOCK = TP * SHARD
 TOKENS = STEPS * ROWS
 CHUNKS = 4
-Z_FIRST = ()
+Z_FIRST = (1,)
 SLOTS = 4
 CROWS = ROWS // CHUNKS
 HALF_ROWS = ROWS // 2
@@ -508,22 +508,21 @@
         start, size = STAGES[stage]
         return partial.at[which, :, pl.ds(half * HALF_ROWS, HALF_ROWS), pl.ds(start, size)]
 
-    def part_go(stage):
+    def part_go(stage, half):
         start, size = STAGES[stage]
-        for half in range(2):
-            for step in range(STEPS):
-                rows = pl.ds(step * ROWS + half * HALF_ROWS, HALF_ROWS)
-                partial[0, step, pl.ds(half * HALF_ROWS, HALF_ROWS), start : start + size] = acc[
-                    1, rows, start : start + size
-                ].astype(jnp.bfloat16)
-            send(
-                part_block(0, stage, half),
-                part_block(1, stage, half),
-                part_send,
-                part_recv,
-                stage * 2 + half,
-                y_dev,
-            )
+        for step in range(STEPS):
+            rows = pl.ds(step * ROWS + half * HALF_ROWS, HALF_ROWS)
+            partial[0, step, pl.ds(half * HALF_ROWS, HALF_ROWS), start : start + size] = acc[
+                1, rows, start : start + size
+            ].astype(jnp.bfloat16)
+        send(
+            part_block(0, stage, half),
+            part_block(1, stage, half),
+            part_send,
+            part_recv,
+            stage * 2 + half,
+            y_dev,
+        )
 
     def part_got(stage, half):
         receive(part_block(1, stage, half), part_send, part_recv, stage * 2 + half)
@@ -569,11 +568,12 @@
         a2a_got(1)
         ring_own(1)
         project(0, 1, far)
-        part_go(0)
+        part_go(0, 0)
         project(0, 0, far)
     with jax.named_scope("project"):
         project(1, 0, x, True)
         project(1, 1, x, True)
+        part_go(0, 1)
 
     def rotate(block, rows):
         return block * cosine[rows, :] + pltpu.roll(block, HD // 2, 1) * sine[rows, :]
@@ -728,33 +728,36 @@
         ring_near(1)
         project(1, 1, west)
         project(1, 1, east)
-        project(1, 0, west)
-        project(1, 0, east)
     with jax.named_scope("ring_far_1"):
         ring_far(1)
+        project(1, 1, far)
+        part_go(1, 0)
         o_on(y, 8)
         o_swapped()
         o_own(1 - y, 12)
-        project(1, 1, far)
-        part_go(1)
-        project(1, 0, far)
     with jax.named_scope("attn_0"):
         first_of_other(0)
     with jax.named_scope("keys"):
         pair_got(1)
-    attend_and_send(1)
+    attend_and_send(1, lambda: part_go(1, 1))
     with jax.named_scope("attn_1"):
         gathers[0].second()
+    with jax.named_scope("project"):
+        project(1, 0, west)
+        project(1, 0, east)
+        project(1, 0, far)
     with jax.named_scope("queries"):
-        for half in range(2):
-            part_got(1, half)
-            place_queries(1, half)
+        part_got(1, 0)
+        place_queries(1, 0)
 
     def between_2():
         with jax.named_scope("attn_2"):
             first_of_other(1)
 
     attend_and_send(2, between_2)
+    with jax.named_scope("queries"):
+        part_got(1, 1)
+        place_queries(1, 1)
 
     def between_3():
         with jax.named_scope("attn_3"):

time: 150 us -> 147 us (0.980)
  Pallas kernels: 145 us -> 143 us
    pallas_call x1, Pallas kernels: 145 us -> 143 us  [per_device(): pl.pallas_call(kernel, out_shape=(jax.ShapeDtypeStruct((STEPS, ROWS, QC),...]
where the time goes in v5:
time: 147 us
  Pallas kernels  143 us (97%)
  local copies, waits for them, and re-layouts  3.54 us (2%)
    pallas_call x1, Pallas kernels, per_device(): pl.pallas_call(kernel, out_shape=(jax.ShapeDtypeStruct((STEPS, ROWS, QC),...  143 us
    unnamed x2, local copies, waits for them, and re-layouts  3.54 us

profile of v5, /device:TPU:1, one launch (start us, length us, event | category | flops | bytes accessed | tf_op | source)
XLA Modules:
  0.0 147.0 jit_solution(10240114501596846270)
XLA Ops:
  0.6 142.8 %shard_map.131 = (bf16[4,128,512]{2,1,0:T(8,128)(2,1)}, bf16[16,8192]{1,0:T(8,128)(2,1)}) custom-call(bf16[4,128,8192]{2,1,0:T(8,128)(2,1)} %hidden.1, bf16[8192]{0:T(1024)(128)(2,1)} %gain.1, bf16[64,8192]{1,0:T(8,128)(2,1)} %q_weight.1, bf16[64,1024]{1,0:T(8,128)(2,1)} %k_weight.1, bf16[64,1024]{1,0:T(8,128)(2,1)} %v_weight.1, bf16[64,8192]{1,0:T(8,128)(2,1)} %o_weight.1, ...), custom_call_target="tpu_custom_call" | custom-call | tf_op jit(solution)/shard_map/pallas_call | solution.py:925
  143.5 1.9 %copy.16 = bf16[4,128,512]{2,1,0:T(8,128)(2,1)} copy(bf16[4,128,512]{2,1,0:T(8,128)(2,1)} %get-tuple-element.4) | data formatting | bytes 1048576
  145.3 1.7 %copy.17 = bf16[16,8192]{1,0:T(8,128)(2,1)} copy(bf16[16,8192]{1,0:T(8,128)(2,1)} %get-tuple-element.5) | data formatting | bytes 524288
